TPU v7x, 32 devices: a whole 2x2x4 slice. The times are simulated.
32 devices in a mesh: gx: 8 (over y, x, core), gy: 4 (over z).
Axes of the slice: x: 2, y: 2, z: 4, core: 2. Of those that a mesh axis runs over, the one named last changes fastest.
Arguments:
- labels: int32 [64, 128, 64], P('gx', 'gy'), may hold values from 0 to 3
- seed_noise: float32 [4, 64, 128, 64], P(None, 'gx', 'gy'), may hold values from 0.05 to 1
- conc: float32 [64, 128, 64], P('gx', 'gy'), may hold values from 0.1 to 0.9
- curvature: float32 [4], replicated, may hold values from 1 to 4
- quartic: float32 [4], replicated, may hold values from 2 to 16
- wells: float32 [4], replicated, may hold values from 0.1 to 0.9
- lame: float32 [2, 4], replicated, may hold values from 0.5 to 2
- eigen: float32 [4, 6], replicated, may hold values from -3 to 3
Outputs:
- phase_next: float32 [4, 64, 128, 64], P(None, 'gx', 'gy')
- conc_next: float32 [64, 128, 64], P('gx', 'gy')
- stress: float32 [6, 64, 128, 64], P(None, 'gx', 'gy')
All inputs are finite; a program needn't handle non-finite values.
Results may differ from a plain program's by a relative error of at most 0.0003.
Values sent between devices are 32-bit elements; how exact they have to be, the bound alone decides.
A program may use at most 128 MiB of HBM per device.

v0:
```python
import math

import jax
import jax.numpy as jnp
from jax import lax
from jax.sharding import PartitionSpec as P

NEWTON = 5
ITERS = 2


step_phase = 0.06
step_conc = 0.005


def with_halo(x, sides, width):
    for axis, dim in sides:
        count, length = (lax.axis_size(axis), x.shape[dim])
        up = [(i, (i + 1) % count) for i in range(count)]
        down = [(j, i) for i, j in up]
        last = lax.slice_in_dim(x, length - width, length, axis=dim)
        initial = lax.slice_in_dim(x, 0, width, axis=dim)
        before = lax.ppermute(last, axis, up)
        after = lax.ppermute(initial, axis, down)
        x = jnp.concatenate([before, x, after], axis=dim)
    return x


def column(values):
    return values.reshape(4, 1, 1, 1)


def phases_from(labels, seed_noise):
    marks = lax.broadcasted_iota(jnp.int32, (4, 1, 1, 1), 0)
    raw = seed_noise + 2.0 * (labels[None] == marks).astype(seed_noise.dtype)
    return raw / jnp.sum(raw, axis=0, keepdims=True)


def partition(phase, conc, curvature, quartic, wells):
    coef_a = column(curvature)
    coef_b = column(quartic)
    centre = column(wells)
    part = jnp.broadcast_to(conc[None], phase.shape)
    deviate = part - centre
    chem = jnp.sum(phase * (coef_a * deviate + coef_b * deviate**3), axis=0)
    for _ in range(NEWTON):
        deviate = part - centre
        slope = coef_a * deviate + coef_b * deviate**3 - chem[None]
        stiff = coef_a + 3.0 * coef_b * deviate * deviate
        shift = (
            conc - jnp.sum(phase * part, axis=0) + jnp.sum(phase * slope / stiff, axis=0)
        ) / jnp.sum(phase / stiff, axis=0)
        part = part + (shift[None] - slope) / stiff
        chem = chem + shift
    return (part, chem)


def stress_of(strain, eigen_field, lam_field, shear_field):
    elastic = strain - eigen_field
    trace = elastic[0] + elastic[1] + elastic[2]
    normal = (lax.broadcasted_iota(jnp.int32, (6, 1, 1, 1), 0) < 3).astype(strain.dtype)
    return 2.0 * shear_field[None] * elastic + (lam_field * trace)[None] * normal


def green(tau, freq_x, freq_y, freq_z, zero, lam0, mu0):
    vec_x = tau[0] * freq_x + tau[5] * freq_y + tau[4] * freq_z
    vec_y = tau[5] * freq_x + tau[1] * freq_y + tau[3] * freq_z
    vec_z = tau[4] * freq_x + tau[3] * freq_y + tau[2] * freq_z
    inner = freq_x * vec_x + freq_y * vec_y + freq_z * vec_z
    square = freq_x * freq_x + freq_y * freq_y + freq_z * freq_z + zero
    first = 1.0 / (2.0 * mu0 * square)
    second = (lam0 + mu0) / (mu0 * (lam0 + 2.0 * mu0)) * inner / (square * square)
    pairs = (
        (freq_x, vec_x, freq_x, vec_x),
        (freq_y, vec_y, freq_y, vec_y),
        (freq_z, vec_z, freq_z, vec_z),
        (freq_y, vec_y, freq_z, vec_z),
        (freq_x, vec_x, freq_z, vec_z),
        (freq_x, vec_x, freq_y, vec_y),
    )
    result = [(fk * vh + fh * vk) * first - fk * fh * second for fk, vk, fh, vh in pairs]
    return jnp.stack(result, axis=0)


def tables(length):
    grid = lax.broadcasted_iota(jnp.int32, (length, length), 0) * lax.broadcasted_iota(
        jnp.int32, (length, length), 1
    )
    angle = (grid % length).astype(jnp.float32) * (2.0 * math.pi / length)
    return (jnp.cos(angle), jnp.sin(angle))


def apply_table(table, data, axis):
    if axis == 3:
        flat = data.reshape(-1, data.shape[3])
        result = jnp.dot(
            flat, table.T, precision=lax.Precision.HIGHEST, preferred_element_type=jnp.float32
        )
        return result.reshape(data.shape[:3] + (table.shape[0],))
    moved = jnp.moveaxis(data, axis, 0)
    rest = moved.shape[1:]
    flat = moved.reshape(moved.shape[0], -1)
    result = jnp.dot(
        table, flat, precision=lax.Precision.HIGHEST, preferred_element_type=jnp.float32
    )
    return jnp.moveaxis(result.reshape((table.shape[0],) + rest), 0, axis)


def transform(pair, axis, inverse):
    real, imag = pair
    length = real.shape[axis]
    cosine, sine = tables(length)
    if inverse:
        new_real = (apply_table(cosine, real, axis) - apply_table(sine, imag, axis)) / length
        new_imag = (apply_table(cosine, imag, axis) + apply_table(sine, real, axis)) / length
    else:
        new_real = apply_table(cosine, real, axis) + apply_table(sine, imag, axis)
        new_imag = apply_table(cosine, imag, axis) - apply_table(sine, real, axis)
    return (new_real, new_imag)


def spectrum(stress):
    length = stress.shape[3]
    cosine, sine = tables(length)
    real = apply_table(cosine, stress, 3)
    imag = -apply_table(sine, stress, 3)
    real, imag = transform(
        (
            lax.all_to_all(real, "gy", split_axis=3, concat_axis=2, tiled=True),
            lax.all_to_all(imag, "gy", split_axis=3, concat_axis=2, tiled=True),
        ),
        axis=2,
        inverse=False,
    )
    real, imag = transform(
        (
            lax.all_to_all(real, "gx", split_axis=2, concat_axis=1, tiled=True),
            lax.all_to_all(imag, "gx", split_axis=2, concat_axis=1, tiled=True),
        ),
        axis=1,
        inverse=False,
    )
    return (real, imag)


def recover(pair):
    pair = transform(pair, 1, True)
    pair = transform(
        (
            lax.all_to_all(pair[0], "gx", split_axis=1, concat_axis=2, tiled=True),
            lax.all_to_all(pair[1], "gx", split_axis=1, concat_axis=2, tiled=True),
        ),
        axis=2,
        inverse=True,
    )
    result = transform(
        (
            lax.all_to_all(pair[0], "gy", split_axis=2, concat_axis=3, tiled=True),
            lax.all_to_all(pair[1], "gy", split_axis=2, concat_axis=3, tiled=True),
        ),
        axis=3,
        inverse=True,
    )
    return result


def frequencies(count, offset, length, axis):
    index = lax.iota(jnp.int32, count) + offset
    index = jnp.where(index >= length // 2, index - length, index)
    kept = jnp.where(index == -(length // 2), 0, index)
    dims_shape = [1, 1, 1]
    dims_shape[axis] = count
    return (kept.astype(jnp.float32) / length).reshape(dims_shape)


def wave_numbers(dims, full_x, full_y, full_z):
    offsets = (jnp.int32(0), lax.axis_index("gx") * dims[2], lax.axis_index("gy") * dims[3])
    freq_x = frequencies(dims[1], offsets[0], full_x, 0)
    freq_y = frequencies(dims[2], offsets[1], full_y, 1)
    freq_z = frequencies(dims[3], offsets[2], full_z, 2)
    zero = ((freq_x == 0.0) & (freq_y == 0.0) & (freq_z == 0.0)).astype(jnp.float32)
    return (freq_x, freq_y, freq_z, zero)


def laplace_padded(padded):
    centre = padded[:, 1:-1, 1:-1, :]
    total = -6.0 * centre
    total = total + padded[:, 2:, 1:-1, :] + padded[:, :-2, 1:-1, :]
    total = total + padded[:, 1:-1, 2:, :] + padded[:, 1:-1, :-2, :]
    total = total + jnp.roll(centre, 1, 3) + jnp.roll(centre, -1, 3)
    return total


def shards(labels, seed_noise, conc, curvature, quartic, wells, lame, eigen):
    phase = phases_from(labels, seed_noise)
    part, chem = partition(phase, conc, curvature, quartic, wells)
    stacked = jnp.concatenate([phase, chem[None]], axis=0)
    padded = with_halo(stacked, (("gx", 1), ("gy", 2)), 1)
    lam_field = jnp.sum(phase * column(lame[0]), axis=0)
    shear_field = jnp.sum(phase * column(lame[1]), axis=0)
    eigen_field = jnp.einsum("ap,axyz->pxyz", eigen, phase, precision=lax.Precision.HIGHEST)
    lam0 = 0.5 * (jnp.max(lame[0]) + jnp.min(lame[0]))
    mu0 = 0.5 * (jnp.max(lame[1]) + jnp.min(lame[1]))
    full_x = labels.shape[0] * lax.axis_size("gx")
    full_y = labels.shape[1] * lax.axis_size("gy")
    full_z = labels.shape[2]
    strain = jnp.zeros((6,) + labels.shape, jnp.float32)
    for _ in range(ITERS):
        stress = stress_of(strain, eigen_field, lam_field, shear_field)
        real, imag = spectrum(stress)
        freq_x, freq_y, freq_z, zero = wave_numbers(real.shape, full_x, full_y, full_z)
        upd_real = green(real, freq_x, freq_y, freq_z, zero, lam0, mu0)
        upd_imag = green(imag, freq_x, freq_y, freq_z, zero, lam0, mu0)
        packed = (upd_real[0::2] - upd_imag[1::2], upd_imag[0::2] + upd_real[1::2])
        back_real, back_imag = recover(packed)
        change = jnp.stack([back_real, back_imag], axis=1).reshape(strain.shape)
        strain = strain - change
    stress = stress_of(strain, eigen_field, lam_field, shear_field)
    deviate = part - column(wells)
    energy = 0.5 * column(curvature) * deviate**2 + 0.25 * column(quartic) * deviate**4
    chemical = energy - chem[None] * part
    elastic = strain - eigen_field
    trace = elastic[0] + elastic[1] + elastic[2]
    squares = (
        elastic[0] ** 2
        + elastic[1] ** 2
        + elastic[2] ** 2
        + 2.0 * (elastic[3] ** 2 + elastic[4] ** 2 + elastic[5] ** 2)
    )
    weight = jnp.array([1.0, 1.0, 1.0, 2.0, 2.0, 2.0], jnp.float32)
    coupling = jnp.einsum(
        "ap,pxyz->axyz", eigen * weight[None], stress, precision=lax.Precision.HIGHEST
    )
    stored = (
        0.5 * (column(lame[0]) * trace[None] ** 2 + 2.0 * column(lame[1]) * squares[None])
        - coupling
    )
    total_sq = jnp.sum(phase * phase, axis=0)
    barrier = 2.0 * phase * (total_sq[None] - phase * phase)
    laplacian = laplace_padded(padded)
    force = chemical + stored + barrier - laplacian[:4]
    phase_next = phase - step_phase * (force - jnp.mean(force, axis=0, keepdims=True))
    conc_next = conc + step_conc * laplacian[4]
    return (phase_next, conc_next, stress)


def solution(mesh):
    in_specs = (
        P("gx", "gy", None),
        P(None, "gx", "gy", None),
        P("gx", "gy", None),
        P(),
        P(),
        P(),
        P(),
        P(),
    )
    out_specs = (P(None, "gx", "gy", None), P("gx", "gy", None), P(None, "gx", "gy", None))
    return jax.shard_map(shards, mesh=mesh, in_specs=in_specs, out_specs=out_specs, check_vma=False)
```

profile of v0, /device:TPU:0, one launch (start us, length us, event | category | flops | bytes accessed | tf_op | source)
XLA Modules:
  0.0 413.2 jit_solution(1960984414806727303)
XLA Ops:
  10.6 2.9 multiply_reduce_fusion.5
  13.6 2.9 multiply_reduce_fusion.4
  16.6 3.4 multiply_reduce_fusion.3
  20.1 4.4 %multiply_reduce_fusion.2 = (f32[8,32,64]{2,1,0:T(8,128)}, f32[8,32,64]{2,1,0:T(8,128)}, f32[8,32,64]{2,1,0:T(8,128)}, f32[8,32,64]{2,1,0:T(8,128)S(1)}, f32[8,32,64]{2,1,0:T(8,128)S(1)}, /*index=5*/f32[4,8,32,64]{3,0,2,1:T(4,128)}) fusion(f32[4,8,32,64]{3,0,2,1:T(4,128)S(1)} %get-tuple-element.68, f32[4]{0:T(128)S(1)} %get-tuple-element.103, ...), kind=kLoop, calls=%fused_computation.159 | loop fusion | flops 2408448 | bytes 1704032 | tf_op jit(solution)/shard_map/reduce_sum | solution.py:51
  27.9 2.9 reshape.486
  30.7 6.3 %all-to-all-start = ((f32[4,1,24576]{2,1,0:T(1,128)}), f32[4,1,24576]{2,1,0:T(1,128)}, u32[]{:S(2)}, u32[]{:S(2)}) async-start(f32[4,1,24576]{2,1,0:T(1,128)} %reshape.486), calls=%async_computation | async-start | bytes 786432 | tf_op jit(solution)/shard_map/all_to_all | solution.py:129
  44.2 4.7 %all-to-all-done = f32[4,1,24576]{2,1,0:T(1,128)} async-done(((f32[4,1,24576]{2,1,0:T(1,128)}), f32[4,1,24576]{2,1,0:T(1,128)}, u32[]{:S(2)}, u32[]{:S(2)}) %all-to-all-start) | async-done | bytes 393248 | tf_op jit(solution)/shard_map/all_to_all | solution.py:129
  48.9 4.3 %all-to-all-start.1 = ((f32[4,1,24576]{2,1,0:T(1,128)}), f32[4,1,24576]{2,1,0:T(1,128)}, u32[]{:S(2)}, u32[]{:S(2)}) async-start(f32[4,1,24576]{2,1,0:T(1,128)} %reshape.488), calls=%async_computation.1 | async-start | bytes 786432 | tf_op jit(solution)/shard_map/all_to_all | solution.py:130
  58.0 3.3 reduce.5
  62.9 2.2 copy.185
  68.7 3.3 reduce.4
  73.5 2.2 copy.188
  78.6 2.2 copy.189
  80.9 3.4 reshape.490
  84.3 4.1 all-to-all-start.2
  89.9 2.2 copy.192
  92.1 3.4 reshape.492
  96.7 3.5 all-to-all-start.3
  102.2 2.7 reshape.491
  104.9 4.6 %copy.190 = f32[6,8,8,16,16]{4,3,1,2,0:T(8,128)} copy(f32[6,8,8,16,16]{4,1,0,3,2:T(8,128)} %bitcast.486) | data formatting | bytes 786432 | tf_op jit(solution)/shard_map/all_to_all | solution.py:137
  109.5 2.5 copy.191
  115.3 2.7 reshape.493
  118.0 4.6 %copy.193 = f32[6,8,8,16,16]{4,3,1,2,0:T(8,128)} copy(f32[6,8,8,16,16]{4,1,0,3,2:T(8,128)} %bitcast.487) | data formatting | bytes 786432 | tf_op jit(solution)/shard_map/all_to_all | solution.py:138
  122.6 2.9 copy.194
  136.8 4.1 %all-to-all-start.4 = ((f32[8,1,6144]{2,1,0:T(1,128)}), f32[8,1,6144]{2,1,0:T(1,128)}, u32[]{:S(2)}, u32[]{:S(2)}) async-start(f32[8,1,6144]{2,1,0:T(1,128)} %reshape.496), calls=%async_computation.4 | async-start | bytes 393216 | tf_op jit(solution)/shard_map/all_to_all | solution.py:150
  140.9 2.6 fusion.17
  147.3 4.2 %all-to-all-start.5 = ((f32[8,1,6144]{2,1,0:T(1,128)}), f32[8,1,6144]{2,1,0:T(1,128)}, u32[]{:S(2)}, u32[]{:S(2)}) async-start(f32[8,1,6144]{2,1,0:T(1,128)} %reshape.494), calls=%async_computation.5 | async-start | bytes 393216 | tf_op jit(solution)/shard_map/all_to_all | solution.py:151
  151.5 2.6 reduce.9
  160.3 2.6 reduce.8
  172.6 5.0 %all-to-all-start.6 = ((f32[4,1,12288]{2,1,0:T(1,128)}), f32[4,1,12288]{2,1,0:T(1,128)}, u32[]{:S(2)}, u32[]{:S(2)}) async-start(f32[4,1,12288]{2,1,0:T(1,128)} %reshape.500), calls=%async_computation.6 | async-start | bytes 393216 | tf_op jit(solution)/shard_map/all_to_all | solution.py:158
  185.9 3.4 all-to-all-start.7
  205.8 2.4 fusion.29
  214.3 2.9 reshape.502
  217.2 5.4 %all-to-all-start.8 = ((f32[4,1,24576]{2,1,0:T(1,128)}), f32[4,1,24576]{2,1,0:T(1,128)}, u32[]{:S(2)}, u32[]{:S(2)}) async-start(f32[4,1,24576]{2,1,0:T(1,128)} %reshape.502), calls=%async_computation.8 | async-start | bytes 786432 | tf_op jit(solution)/shard_map/all_to_all | solution.py:129
  229.5 5.6 %all-to-all-done.8 = f32[4,1,24576]{2,1,0:T(1,128)} async-done(((f32[4,1,24576]{2,1,0:T(1,128)}), f32[4,1,24576]{2,1,0:T(1,128)}, u32[]{:S(2)}, u32[]{:S(2)}) %all-to-all-start.8) | async-done | bytes 393248 | tf_op jit(solution)/shard_map/all_to_all | solution.py:129
  235.1 4.1 all-to-all-start.9
  244.8 3.8 collective-permute-start.2
  248.6 3.3 reduce.13
  253.5 2.2 copy.212
  259.3 3.3 reduce.12
  264.1 2.2 copy.215
  269.2 2.2 copy.216
  271.4 3.4 reshape.506
  274.9 4.1 all-to-all-start.10
  280.5 2.2 copy.219
  282.7 3.5 reshape.508
  287.3 4.1 all-to-all-start.11
  291.4 4.4 %fusion.48 = f32[5,8,32,64]{3,0,2,1:T(8,128)} fusion(f32[1,8,32,64]{3,0,2,1:T(1,128)S(1)} %bitcast.532, f32[4,8,32,64]{3,0,2,1:T(4,128)S(1)} %get-tuple-element.68, f32[5,10,1,64]{3,0,2,1:T(8,128)} %collective-permute-done.3, f32[5,1,32,64]{3,0,2,1:T(8,128)} %collective-permute-done, f32[5,1,32,64]{3,0,2,1:T(8,128)} %collective-permute-done.1, ...), kind=kLoop, calls=%fused_computation.89 | loop fusion | flops 1802240 | bytes 1418240 | tf_op jit(solution)/shard_map/add | solution.py:190
  297.3 2.7 reshape.507
  300.0 4.6 %copy.217 = f32[6,8,8,16,16]{4,3,1,2,0:T(8,128)} copy(f32[6,8,8,16,16]{4,1,0,3,2:T(8,128)} %bitcast.490) | data formatting | bytes 786432 | tf_op jit(solution)/shard_map/all_to_all | solution.py:137
  304.6 2.5 copy.218
  308.9 2.5 reduce.14
  311.4 2.7 reshape.509
  314.1 4.6 %copy.220 = f32[6,8,8,16,16]{4,3,1,2,0:T(8,128)} copy(f32[6,8,8,16,16]{4,1,0,3,2:T(8,128)} %bitcast.491) | data formatting | bytes 786432 | tf_op jit(solution)/shard_map/all_to_all | solution.py:138
  318.7 2.7 copy.221
  332.5 4.1 all-to-all-start.12
  336.6 2.6 fusion.21
  343.0 4.4 %all-to-all-start.13 = ((f32[8,1,6144]{2,1,0:T(1,128)}), f32[8,1,6144]{2,1,0:T(1,128)}, u32[]{:S(2)}, u32[]{:S(2)}) async-start(f32[8,1,6144]{2,1,0:T(1,128)} %reshape.510), calls=%async_computation.13 | async-start | bytes 393216 | tf_op jit(solution)/shard_map/all_to_all | solution.py:151
  347.4 2.6 reduce.17
  356.3 2.6 reduce.16
  368.6 5.1 %all-to-all-start.14 = ((f32[4,1,12288]{2,1,0:T(1,128)}), f32[4,1,12288]{2,1,0:T(1,128)}, u32[]{:S(2)}, u32[]{:S(2)}) async-start(f32[4,1,12288]{2,1,0:T(1,128)} %reshape.516), calls=%async_computation.14 | async-start | bytes 393216 | tf_op jit(solution)/shard_map/all_to_all | solution.py:158
  381.8 3.5 all-to-all-start.15
  401.4 2.4 fusion.25
  409.2 2.7 fusion.493
  (338 shorter events, 190.3 us)
Async XLA Ops:
  0.6 6.7 %copy-start.71 = (f32[4,6]{1,0:T(4,128)S(1)}, f32[4,6]{1,0:T(4,128)}, u32[]{:S(2)}) copy-start(f32[4,6]{1,0:T(4,128)} %param.16) | copy-start | bytes 292
  0.7 36.4 %copy-start.63 = (f32[6]{0:T(128)}, f32[6]{0:T(128)S(1)}, u32[]{:S(2)}) copy-start(f32[6]{0:T(128)S(1)} %compare_convert_fusion) | copy-start | bytes 76
  1.8 18.2 %copy-start.61 = (f32[4]{0:T(128)}, f32[4]{0:T(128)S(1)}, u32[]{:S(2)}) copy-start(f32[4]{0:T(128)S(1)} %get-tuple-element.103) | copy-start | bytes 52
  3.3 16.8 %copy-start.73 = (f32[4]{0:T(128)}, f32[4]{0:T(128)S(1)}, u32[]{:S(2)}) copy-start(f32[4]{0:T(128)S(1)} %get-tuple-element.101) | copy-start | bytes 52
  20.1 4.4 %copy-start.26 = (f32[8,32,64]{2,1,0:T(8,128)}, f32[8,32,64]{2,1,0:T(8,128)S(1)}, u32[]{:S(2)}) copy-start(f32[8,32,64]{2,1,0:T(8,128)S(1)} %get-tuple-element.58) | copy-start | bytes 196612
  30.7 18.1 %all-to-all-start = ((f32[4,1,24576]{2,1,0:T(1,128)}), f32[4,1,24576]{2,1,0:T(1,128)}, u32[]{:S(2)}, u32[]{:S(2)}) async-start(f32[4,1,24576]{2,1,0:T(1,128)} %reshape.486), calls=%async_computation | async-start | bytes 786432 | tf_op jit(solution)/shard_map/all_to_all | solution.py:129
  38.9 3.4 copy-start.58
  38.9 4.6 %copy-start.38 = (f32[64]{0:T(128)}, f32[64]{0:T(128)S(1)}, u32[]{:S(2)}) copy-start(f32[64]{0:T(128)S(1)} %get-tuple-element.112) | copy-start | bytes 772
  38.9 3.4 copy-start.67
  42.8 6.0 %copy-start.34 = (f32[16]{0:T(128)}, f32[16]{0:T(128)S(1)}, u32[]{:S(2)}) copy-start(f32[16]{0:T(128)S(1)} %get-tuple-element.108) | copy-start | bytes 196
  48.9 19.8 %all-to-all-start.1 = ((f32[4,1,24576]{2,1,0:T(1,128)}), f32[4,1,24576]{2,1,0:T(1,128)}, u32[]{:S(2)}, u32[]{:S(2)}) async-start(f32[4,1,24576]{2,1,0:T(1,128)} %reshape.488), calls=%async_computation.1 | async-start | bytes 786432 | tf_op jit(solution)/shard_map/all_to_all | solution.py:130
  75.8 2.1 copy-start.23
  84.3 4.8 %copy-start.11 = (f32[6,8,128,16]{2,3,1,0:T(8,128)S(1)}, f32[6,8,128,16]{2,3,1,0:T(8,128)}, u32[]{:S(2)}) copy-start(f32[6,8,128,16]{2,3,1,0:T(8,128)} %copy-done.10) | copy-start | bytes 1179652
  84.3 12.4 %all-to-all-start.2 = ((f32[8,1,12288]{2,1,0:T(1,128)}), f32[8,1,12288]{2,1,0:T(1,128)S(1)}, u32[]{:S(2)}, u32[]{:S(2)}) async-start(f32[8,1,12288]{2,1,0:T(1,128)} %reshape.490), calls=%async_computation.2 | async-start | bytes 786432 | tf_op jit(solution)/shard_map/all_to_all | solution.py:137
  96.7 17.1 %all-to-all-start.3 = ((f32[8,1,12288]{2,1,0:T(1,128)}), f32[8,1,12288]{2,1,0:T(1,128)S(1)}, u32[]{:S(2)}, u32[]{:S(2)}) async-start(f32[8,1,12288]{2,1,0:T(1,128)} %reshape.492), calls=%async_computation.3 | async-start | bytes 786432 | tf_op jit(solution)/shard_map/all_to_all | solution.py:138
  130.5 2.0 copy-start.7
  130.5 2.0 copy-start.9
  136.8 10.5 %all-to-all-start.4 = ((f32[8,1,6144]{2,1,0:T(1,128)}), f32[8,1,6144]{2,1,0:T(1,128)}, u32[]{:S(2)}, u32[]{:S(2)}) async-start(f32[8,1,6144]{2,1,0:T(1,128)} %reshape.496), calls=%async_computation.4 | async-start | bytes 393216 | tf_op jit(solution)/shard_map/all_to_all | solution.py:150
  147.3 13.1 %all-to-all-start.5 = ((f32[8,1,6144]{2,1,0:T(1,128)}), f32[8,1,6144]{2,1,0:T(1,128)}, u32[]{:S(2)}, u32[]{:S(2)}) async-start(f32[8,1,6144]{2,1,0:T(1,128)} %reshape.494), calls=%async_computation.5 | async-start | bytes 393216 | tf_op jit(solution)/shard_map/all_to_all | solution.py:151
  166.1 2.6 copy-start.31
  172.6 13.2 %all-to-all-start.6 = ((f32[4,1,12288]{2,1,0:T(1,128)}), f32[4,1,12288]{2,1,0:T(1,128)}, u32[]{:S(2)}, u32[]{:S(2)}) async-start(f32[4,1,12288]{2,1,0:T(1,128)} %reshape.500), calls=%async_computation.6 | async-start | bytes 393216 | tf_op jit(solution)/shard_map/all_to_all | solution.py:158
  185.9 13.9 %all-to-all-start.7 = ((f32[4,1,12288]{2,1,0:T(1,128)}), f32[4,1,12288]{2,1,0:T(1,128)S(1)}, u32[]{:S(2)}, u32[]{:S(2)}) async-start(f32[4,1,12288]{2,1,0:T(1,128)} %reshape.498), calls=%async_computation.7 | async-start | bytes 393216 | tf_op jit(solution)/shard_map/all_to_all | solution.py:159
  190.0 53.5 %collective-permute-start = (f32[5,1,32,64]{3,0,2,1:T(8,128)}, f32[5,1,32,64]{3,0,2,1:T(8,128)}, u32[]{:S(2)}, u32[]{:S(2)}) collective-permute-start(f32[5,1,32,64]{3,0,2,1:T(8,128)} %get-tuple-element.79), channel_id=1, source_target_pairs={{4,0},{8,4},{12,8},{16,12},{20,16},{24,20},{28,24},{0,28},{5,1},{9... | collective-permute-start | bytes 122888 | tf_op jit(solution)/shard_map/ppermute | solution.py:24
  191.8 51.7 %collective-permute-start.1 = (f32[5,1,32,64]{3,0,2,1:T(8,128)}, f32[5,1,32,64]{3,0,2,1:T(8,128)}, u32[]{:S(2)}, u32[]{:S(2)}) collective-permute-start(f32[5,1,32,64]{3,0,2,1:T(8,128)} %get-tuple-element.78), channel_id=1, source_target_pairs={{0,4},{4,8},{8,12},{12,16},{16,20},{20,24},{24,28},{28,0},{1,5},{5... | collective-permute-start | bytes 122888 | tf_op jit(solution)/shard_map/ppermute | solution.py:23
  209.9 1.7 copy-start.64
  214.3 8.3 %copy-start.52 = (f32[4]{0:T(128)S(1)}, f32[4]{0:T(128)}, u32[]{:S(2)}) copy-start(f32[4]{0:T(128)} %param.12) | copy-start | bytes 52
  214.3 8.3 %copy-start.70 = (f32[2,4]{1,0:T(2,128)S(1)}, f32[2,4]{1,0:T(2,128)}, u32[]{:S(2)}) copy-start(f32[2,4]{1,0:T(2,128)} %param.15) | copy-start | bytes 100
  217.2 7.2 %copy-start.29 = (f32[8,32,64]{2,1,0:T(8,128)S(1)}, f32[8,32,64]{2,1,0:T(8,128)}, u32[]{:S(2)}) copy-start(f32[8,32,64]{2,1,0:T(8,128)} %copy-done.28) | copy-start | bytes 196612
  217.2 7.2 %copy-start.65 = (f32[6]{0:T(128)S(1)}, f32[6]{0:T(128)}, u32[]{:S(2)}) copy-start(f32[6]{0:T(128)} %copy-done.63) | copy-start | bytes 76
  217.2 17.9 %all-to-all-start.8 = ((f32[4,1,24576]{2,1,0:T(1,128)}), f32[4,1,24576]{2,1,0:T(1,128)}, u32[]{:S(2)}, u32[]{:S(2)}) async-start(f32[4,1,24576]{2,1,0:T(1,128)} %reshape.502), calls=%async_computation.8 | async-start | bytes 786432 | tf_op jit(solution)/shard_map/all_to_all | solution.py:129
  235.1 24.2 %all-to-all-start.9 = ((f32[4,1,24576]{2,1,0:T(1,128)}), f32[4,1,24576]{2,1,0:T(1,128)}, u32[]{:S(2)}, u32[]{:S(2)}) async-start(f32[4,1,24576]{2,1,0:T(1,128)} %reshape.504), calls=%async_computation.9 | async-start | bytes 786432 | tf_op jit(solution)/shard_map/all_to_all | solution.py:130
  244.8 46.5 %collective-permute-start.2 = (f32[5,10,1,64]{3,0,2,1:T(8,128)}, f32[5,10,1,64]{3,0,2,1:T(8,128)}, u32[]{:S(2)}, u32[]{:S(2)}) collective-permute-start(f32[5,10,1,64]{3,0,2,1:T(8,128)} %get-tuple-element.69), channel_id=1, source_target_pairs={{1,0},{2,1},{3,2},{0,3},{5,4},{6,5},{7,6},{4,7},{9,8},{10,9},{11,1... | collective-permute-start | bytes 38408 | tf_op jit(solution)/shard_map/ppermute | solution.py:24
  248.6 42.8 %collective-permute-start.3 = (f32[5,10,1,64]{3,0,2,1:T(8,128)}, f32[5,10,1,64]{3,0,2,1:T(8,128)}, u32[]{:S(2)}, u32[]{:S(2)}) collective-permute-start(f32[5,10,1,64]{3,0,2,1:T(8,128)} %get-tuple-element.70), channel_id=1, source_target_pairs={{0,1},{1,2},{2,3},{3,0},{4,5},{5,6},{6,7},{7,4},{8,9},{9,10},{10,1... | collective-permute-start | bytes 38408 | tf_op jit(solution)/shard_map/ppermute | solution.py:23
  257.8 1.5 copy-start.12
  266.3 2.1 copy-start.24
  274.9 4.8 %copy-start.13 = (f32[6,8,128,16]{2,3,1,0:T(8,128)S(1)}, f32[6,8,128,16]{2,3,1,0:T(8,128)}, u32[]{:S(2)}) copy-start(f32[6,8,128,16]{2,3,1,0:T(8,128)} %copy-done.12) | copy-start | bytes 1179652
  274.9 12.4 %all-to-all-start.10 = ((f32[8,1,12288]{2,1,0:T(1,128)}), f32[8,1,12288]{2,1,0:T(1,128)S(1)}, u32[]{:S(2)}, u32[]{:S(2)}) async-start(f32[8,1,12288]{2,1,0:T(1,128)} %reshape.506), calls=%async_computation.10 | async-start | bytes 786432 | tf_op jit(solution)/shard_map/all_to_all | solution.py:137
  282.7 8.7 %copy-start.5 = (f32[5,8,32,1]{3,0,2,1:T(8,128)S(1)}, f32[5,8,32,1]{3,0,2,1:T(8,128)}, u32[]{:S(2)}) copy-start(f32[5,8,32,1]{3,0,2,1:T(8,128)} %get-tuple-element.76) | copy-start | bytes 15364
  287.3 21.6 %all-to-all-start.11 = ((f32[8,1,12288]{2,1,0:T(1,128)}), f32[8,1,12288]{2,1,0:T(1,128)}, u32[]{:S(2)}, u32[]{:S(2)}) async-start(f32[8,1,12288]{2,1,0:T(1,128)} %reshape.508), calls=%async_computation.11 | async-start | bytes 786432 | tf_op jit(solution)/shard_map/all_to_all | solution.py:138
  321.5 2.0 copy-start.36
  321.5 2.0 copy-start.40
  321.5 2.0 copy-start.42
  321.5 2.0 copy-start.44
  321.5 2.0 copy-start.60
  326.2 2.0 copy-start.6
  326.2 2.0 copy-start.8
  332.5 10.4 %all-to-all-start.12 = ((f32[8,1,6144]{2,1,0:T(1,128)}), f32[8,1,6144]{2,1,0:T(1,128)}, u32[]{:S(2)}, u32[]{:S(2)}) async-start(f32[8,1,6144]{2,1,0:T(1,128)} %reshape.512), calls=%async_computation.12 | async-start | bytes 393216 | tf_op jit(solution)/shard_map/all_to_all | solution.py:150
  343.0 13.3 %all-to-all-start.13 = ((f32[8,1,6144]{2,1,0:T(1,128)}), f32[8,1,6144]{2,1,0:T(1,128)}, u32[]{:S(2)}, u32[]{:S(2)}) async-start(f32[8,1,6144]{2,1,0:T(1,128)} %reshape.510), calls=%async_computation.13 | async-start | bytes 393216 | tf_op jit(solution)/shard_map/all_to_all | solution.py:151
  362.0 2.6 copy-start.32
  368.6 13.3 %all-to-all-start.14 = ((f32[4,1,12288]{2,1,0:T(1,128)}), f32[4,1,12288]{2,1,0:T(1,128)}, u32[]{:S(2)}, u32[]{:S(2)}) async-start(f32[4,1,12288]{2,1,0:T(1,128)} %reshape.516), calls=%async_computation.14 | async-start | bytes 393216 | tf_op jit(solution)/shard_map/all_to_all | solution.py:158
  381.8 13.4 %all-to-all-start.15 = ((f32[4,1,12288]{2,1,0:T(1,128)}), f32[4,1,12288]{2,1,0:T(1,128)S(1)}, u32[]{:S(2)}, u32[]{:S(2)}) async-start(f32[4,1,12288]{2,1,0:T(1,128)} %reshape.514), calls=%async_computation.15 | async-start | bytes 393216 | tf_op jit(solution)/shard_map/all_to_all | solution.py:159
  407.2 1.6 copy-start.37
  407.2 1.6 copy-start.53
  407.2 1.6 copy-start.55
  407.3 1.6 copy-start.57
  407.3 1.5 copy-start.62
  407.3 1.5 copy-start.72
  407.3 1.5 copy-start.74
  407.3 1.5 copy-start.75
  407.3 1.5 copy-start.76
  407.3 1.5 copy-start.77
  407.3 1.5 copy-start.78
  407.3 1.9 copy-start.79
  407.7 4.3 %copy-start.30 = (f32[6,8,32,64]{3,2,1,0:T(8,128)}, f32[6,8,32,64]{3,2,1,0:T(8,128)S(1)}, u32[]{:S(2)}) copy-start(f32[6,8,32,64]{3,2,1,0:T(8,128)S(1)} %multiply_add_fusion) | copy-start | bytes 1179652
  (36 other events, 37.1 us)
where the time goes:
time: 421 us; the launch traced here: 413 us
  local copies, waits for them, and re-layouts  168 us (40%)
  other arithmetic  83.2 us (20%)
  starting transfers between devices  75.5 us (18%)
  matrix products  64.3 us (15%)
  waiting for transfers between devices  17.7 us (4%)
  between operations  4.92 us (1%)
    unnamed x193, local copies, waits for them, and re-layouts  70.3 us
    dot_general x32, matrix products, apply_table(): jnp.dot(table, flat, precision=lax.Precision.HIGHEST, preferred_element_t...  40.5 us
    dot_general x12, matrix products, apply_table(): jnp.dot(flat, table.T, precision=lax.Precision.HIGHEST, preferred_element...  20.1 us
    reduce_sum x5, other arithmetic, partition(): jnp.sum(phase * part, axis=0)  15.5 us
    all_to_all x2, starting transfers between devices, spectrum(): lax.all_to_all(real, 'gy', split_axis=3, concat_axis=2, tiled=True)  11.7 us
    transpose x4, local copies, waits for them, and re-layouts, apply_table(): moved = jnp.moveaxis(data, axis, 0)  10.7 us
    all_to_all x2, waiting for transfers between devices, spectrum(): lax.all_to_all(real, 'gy', split_axis=3, concat_axis=2, tiled=True)  10.3 us
    all_to_all x2, starting transfers between devices, recover(): lax.all_to_all(pair[0], 'gy', split_axis=2, concat_axis=3, tiled=True)  10.1 us
  transfers between devices with their start and end apart: 20, of which 8 were waited for; matrix products, arithmetic and copies ran while one was open for 41% of the time, Pallas kernels for 0%

commit v1 on v0

--- a/solution.py
+++ b/solution.py
@@ -1,8 +1,12 @@
+import functools
 import math
 
 import jax
 import jax.numpy as jnp
+import numpy as np
 from jax import lax
+from jax.experimental import pallas as pl
+from jax.experimental.pallas import tpu as pltpu
 from jax.sharding import PartitionSpec as P
 
 NEWTON = 5
@@ -182,6 +186,448 @@
     return (freq_x, freq_y, freq_z, zero)
 
 
+def slots_fit(full_z):
+    count = lax.axis_size("gx") * lax.axis_size("gy")
+    return full_z % 2 == 0 and (full_z // 2) % count == 0
+
+
+def angles(length):
+    grid = np.outer(np.arange(length), np.arange(length)) % length
+    return grid * (2.0 * math.pi / length)
+
+
+def z_tables(length):
+    half = length // 2
+    angle = angles(length)[:half]
+    real = np.cos(angle)
+    imag = -np.sin(angle)
+    imag[0] = np.cos(math.pi * np.arange(length))
+    forward = np.stack([real, imag], axis=1).astype(np.float32)
+    weight = np.full((half, 1, 1), 2.0 / length)
+    weight[0] = 1.0 / length
+    return forward, (np.stack([real, imag], axis=1) * weight).astype(np.float32)
+
+
+def complex_table(length, inverse):
+    angle = angles(length)
+    cosine, sine = np.cos(angle), np.sin(angle)
+    if inverse:
+        table = np.array([[cosine, -sine], [sine, cosine]]) / length
+    else:
+        table = np.array([[cosine, sine], [-sine, cosine]])
+    return table.transpose(0, 2, 1, 3).astype(np.float32)
+
+
+def contract(spec, *operands):
+    return jnp.einsum(
+        spec, *operands, precision=lax.Precision.HIGH, preferred_element_type=jnp.float32
+    )
+
+
+def fluctuation(stress, full_x, full_y, full_z, lam0, mu0):
+    count_x, count_y = lax.axis_size("gx"), lax.axis_size("gy")
+    count = count_x * count_y
+    _, size_x, size_y, _ = stress.shape
+    slots = full_z // 2 // count
+    forward_z, inverse_z = z_tables(full_z)
+    data = contract("krz,cxyz->krcxy", forward_z, stress)
+    data = lax.all_to_all(data, ("gx", "gy"), split_axis=0, concat_axis=0, tiled=True)
+    data = data.reshape(count_x, count_y, slots, 2, 6, size_x, size_y)
+    data = data.transpose(2, 3, 4, 0, 5, 1, 6).reshape(slots, 2, 6, full_x, full_y)
+    data = contract("sLrl,krcly->kscLy", complex_table(full_x, False), data)
+    data = contract("sLrl,krcxl->kscxL", complex_table(full_y, False), data)
+    data = data.transpose(2, 1, 3, 4, 0)
+    freq_x = frequencies(full_x, 0, full_x, 0)
+    freq_y = frequencies(full_y, 0, full_y, 1)
+    position = lax.axis_index("gx") * count_y + lax.axis_index("gy")
+    freq_z = frequencies(slots, position * slots, full_z, 2)
+    zero = ((freq_x == 0.0) & (freq_y == 0.0) & (freq_z == 0.0)).astype(jnp.float32)
+    data = jnp.stack([green(data[:, r], freq_x, freq_y, freq_z, zero, lam0, mu0) for r in (0, 1)], 1)
+    data = data.transpose(4, 1, 0, 2, 3)
+    data = contract("sLrl,krcxl->kscxL", complex_table(full_y, True), data)
+    data = contract("sLrl,krcly->kscLy", complex_table(full_x, True), data)
+    data = data.reshape(slots, 2, 6, count_x, size_x, count_y, size_y)
+    data = data.transpose(3, 5, 0, 1, 2, 4, 6).reshape(count * slots, 2, 6, size_x, size_y)
+    data = lax.all_to_all(data, ("gx", "gy"), split_axis=0, concat_axis=0, tiled=True)
+    return contract("krz,krcxy->cxyz", inverse_z, data)
+
+
+def fluctuation_general(stress, full_x, full_y, full_z, lam0, mu0):
+    real, imag = spectrum(stress)
+    freq_x, freq_y, freq_z, zero = wave_numbers(real.shape, full_x, full_y, full_z)
+    upd_real = green(real, freq_x, freq_y, freq_z, zero, lam0, mu0)
+    upd_imag = green(imag, freq_x, freq_y, freq_z, zero, lam0, mu0)
+    packed = (upd_real[0::2] - upd_imag[1::2], upd_imag[0::2] + upd_real[1::2])
+    back_real, back_imag = recover(packed)
+    return jnp.stack([back_real, back_imag], axis=1).reshape(stress.shape)
+
+
+MESH = pl.DeviceIdType.MESH
+LANES = 128
+ROWS = 8
+
+
+def kernel_fits(shape):
+    count_x, count_y = lax.axis_size("gx"), lax.axis_size("gy")
+    size_x, size_y, full_z = shape
+    return (
+        full_z == 2 * count_x * count_y
+        and count_x == ROWS
+        and count_y * size_y == LANES
+        and size_x * size_y == 2 * LANES
+        and (count_x * count_y) % 16 == 0
+    )
+
+
+def split(value):
+    high = value.astype(jnp.bfloat16)
+    return high, (value - high.astype(jnp.float32)).astype(jnp.bfloat16)
+
+
+def split_table(table):
+    high = np.asarray(table, np.float32).astype(jnp.bfloat16)
+    low = (np.asarray(table, np.float64) - high.astype(np.float64)).astype(jnp.bfloat16)
+    return high, low
+
+
+def table_left(table):
+    high, low = split_table(table)
+    return np.concatenate([high, high, low], axis=1)
+
+
+def table_right(table):
+    high, low = split_table(table)
+    return np.stack([high, low])
+
+
+def left_product(table, value):
+    high, low = split(value)
+    stacked = jnp.concatenate([high, low, high], axis=0)
+    return jnp.dot(table, stacked, preferred_element_type=jnp.float32)
+
+
+def right_product(value, table):
+    high, low = split(value)
+    product = functools.partial(jnp.dot, preferred_element_type=jnp.float32)
+    return product(high, table[0]) + (product(low, table[0]) + product(high, table[1]))
+
+
+def kernel_tables(size_x, full_x, full_y, full_z):
+    forward, inverse = z_tables(full_z)
+    forward = forward.transpose(1, 0, 2).reshape(full_z, full_z)
+    inverse = inverse.transpose(2, 1, 0).reshape(full_z, full_z)
+    count_x = full_x // size_x
+    order = np.arange(full_x).reshape(count_x, size_x).T.reshape(-1)
+    to_x = complex_table(full_x, False).transpose(0, 1, 2, 3)
+    forward_x = to_x.transpose(0, 1, 2, 3)[:, :, :, order]
+    inverse_x = complex_table(full_x, True)[:, order]
+    forward_y = complex_table(full_y, False)
+    inverse_y = complex_table(full_y, True)
+    flat = lambda table, length: table.reshape(2 * length, 2 * length)
+    return (
+        table_left(forward),
+        table_left(flat(forward_x, full_x)),
+        table_right(flat(forward_y, full_y).T),
+        table_right(flat(inverse_y, full_y).T),
+        table_left(flat(inverse_x, full_x)),
+        table_left(inverse),
+    )
+
+
+def position():
+    return lax.axis_index("gx") * lax.axis_size("gy") + lax.axis_index("gy")
+
+
+def coordinates(index):
+    count_y = lax.axis_size("gy")
+    return (index // count_y, index % count_y)
+
+
+def greet():
+    count = lax.axis_size("gx") * lax.axis_size("gy")
+    me = position()
+    barrier = pltpu.get_barrier_semaphore()
+
+    def hello(step, carry):
+        other = lax.rem(me + step, count)
+        pl.semaphore_signal(barrier, inc=1, device_id=coordinates(other), device_id_type=MESH)
+        return carry
+
+    lax.fori_loop(1, count, hello, 0)
+    pl.semaphore_wait(barrier, count - 1)
+
+
+def exchange_copy(sent, received, send_sem, recv_sem, source, target):
+    rows = sent.shape[0] // (lax.axis_size("gx") * lax.axis_size("gy"))
+    return pltpu.make_async_remote_copy(
+        src_ref=sent.at[pl.ds(pl.multiple_of(target * rows, 8), rows)],
+        dst_ref=received.at[pl.ds(pl.multiple_of(source * rows, 8), rows)],
+        send_sem=send_sem.at[target],
+        recv_sem=recv_sem.at[source],
+        device_id=coordinates(target),
+        device_id_type=MESH,
+    )
+
+
+def exchange_start(sent, received, send_sem, recv_sem):
+    count = lax.axis_size("gx") * lax.axis_size("gy")
+    me = position()
+    rows = sent.shape[0] // count
+
+    def send(step, carry):
+        target = lax.rem(me + step, count)
+        exchange_copy(sent, received, send_sem, recv_sem, me, target).start()
+        return carry
+
+    lax.fori_loop(1, count, send, 0)
+    own = pl.ds(pl.multiple_of(me * rows, 8), rows)
+    received[own, :] = sent[own, :]
+
+
+def exchange_wait(sent, received, send_sem, recv_sem, arrived):
+    count = lax.axis_size("gx") * lax.axis_size("gy")
+    me = position()
+
+    def wait(step, carry):
+        other = lax.rem(me + step, count)
+        if arrived:
+            exchange_copy(sent, received, send_sem, recv_sem, other, other).wait_recv()
+        else:
+            exchange_copy(sent, received, send_sem, recv_sem, me, other).wait_send()
+        return carry
+
+    lax.fori_loop(1, count, wait, 0)
+
+
+def swap_blocks(parts):
+    count = len(parts)
+    width = LANES // count
+    block = lax.broadcasted_iota(jnp.int32, parts[0].shape, 1) // width
+    result = []
+    for a in range(count):
+        total = None
+        for b, part in enumerate(parts):
+            shift = (width * (b - a)) % LANES
+            moved = pltpu.roll(part, shift, 1) if shift else part
+            total = moved if total is None else jnp.where(block == b, moved, total)
+        result.append(total)
+    return result
+
+
+def halves(z_ref, t_ref, sent):
+    slots = z_ref.shape[0] // 2
+    rows = 4 * 6
+    for c in range(6):
+        result = left_product(z_ref[...], t_ref[c])
+        for r in range(2):
+            for h in range(2):
+                piece = result[r * slots:(r + 1) * slots, h * LANES:(h + 1) * LANES]
+                sent[pl.ds(c * 4 + r * 2 + h, slots, stride=rows), :] = piece
+
+
+def plane_rows(received, c, r, count_y):
+    rows = 4 * 6
+    result = []
+    for h in range(2):
+        first = c * 4 + r * 2 + h
+        parts = [
+            received[pl.ds(j * rows + first, ROWS, stride=rows * count_y), :]
+            for j in range(count_y)
+        ]
+        result += swap_blocks(parts)
+    return jnp.concatenate(result, axis=0)
+
+
+def plane_store(sent, value, c, r, count_y):
+    rows = 4 * 6
+    for h in range(2):
+        first = c * 4 + r * 2 + h
+        parts = [
+            value[(h * count_y + a) * ROWS:(h * count_y + a + 1) * ROWS] for a in range(count_y)
+        ]
+        for j, part in enumerate(swap_blocks(parts)):
+            sent[pl.ds(j * rows + first, ROWS, stride=rows * count_y), :] = part
+
+
+def plane_green(received, sent, fx_ref, fy_ref, iy_ref, ix_ref, coefs, full_x, full_y, full_z):
+    count_y = lax.axis_size("gy")
+    rows_x = []
+    for c in range(6):
+        both = [plane_rows(received, c, r, count_y) for r in range(2)]
+        rows_x.append(jnp.concatenate(both, axis=0))
+    spec = left_product(fx_ref[...], jnp.concatenate(rows_x, axis=1))
+    lanes = []
+    for c in range(6):
+        part = spec[:, c * full_y:(c + 1) * full_y]
+        lanes.append(jnp.concatenate([part[:full_x], part[full_x:]], axis=1))
+    spec = right_product(jnp.concatenate(lanes, axis=0), fy_ref)
+    first, second, freq_x, freq_y, freq_z = coefs
+    tau = [spec[c * full_x:(c + 1) * full_x] for c in range(6)]
+    vec_x = tau[0] * freq_x + tau[5] * freq_y + tau[4] * freq_z
+    vec_y = tau[5] * freq_x + tau[1] * freq_y + tau[3] * freq_z
+    vec_z = tau[4] * freq_x + tau[3] * freq_y + tau[2] * freq_z
+    inner = (freq_x * vec_x + freq_y * vec_y + freq_z * vec_z) * second
+    pairs = (
+        (freq_x, vec_x, freq_x, vec_x),
+        (freq_y, vec_y, freq_y, vec_y),
+        (freq_z, vec_z, freq_z, vec_z),
+        (freq_y, vec_y, freq_z, vec_z),
+        (freq_x, vec_x, freq_z, vec_z),
+        (freq_x, vec_x, freq_y, vec_y),
+    )
+    spec = [(fk * vh + fh * vk) * first - fk * fh * inner for fk, vk, fh, vh in pairs]
+    spec = right_product(jnp.concatenate(spec, axis=0), iy_ref)
+    lanes = []
+    for c in range(6):
+        part = spec[c * full_x:(c + 1) * full_x]
+        lanes.append(jnp.concatenate([part[:, :full_y], part[:, full_y:]], axis=0))
+    plane = left_product(ix_ref[...], jnp.concatenate(lanes, axis=1))
+    for c in range(6):
+        for r in range(2):
+            value = plane[r * full_x:(r + 1) * full_x, c * full_y:(c + 1) * full_y]
+            plane_store(sent, value, c, r, count_y)
+
+
+def wave_parts(lame_ref, full_x, full_y, full_z):
+    shape = (full_x, 2 * full_y)
+    row = lax.broadcasted_iota(jnp.int32, shape, 0)
+    lane = lax.broadcasted_iota(jnp.int32, shape, 1) % full_y
+
+    def weight(index, length):
+        signed = jnp.where(index >= length // 2, index - length, index)
+        signed = jnp.where(signed == -(length // 2), 0, signed)
+        return signed.astype(jnp.float32) * (1.0 / length)
+
+    freq_x = weight(row, full_x)
+    freq_y = weight(lane, full_y)
+    freq_z = weight(jnp.full(shape, position(), jnp.int32), full_z)
+    square = freq_x * freq_x + freq_y * freq_y + freq_z * freq_z
+    square = jnp.where(square == 0.0, 1.0, square)
+
+    def middle(which):
+        values = [jnp.full(shape, lame_ref[which, a], jnp.float32) for a in range(4)]
+        top = functools.reduce(jnp.maximum, values)
+        return 0.5 * (top + functools.reduce(jnp.minimum, values))
+
+    lam0, mu0 = middle(0), middle(1)
+    first = 1.0 / (2.0 * mu0 * square)
+    second = (lam0 + mu0) / (mu0 * (lam0 + 2.0 * mu0)) / (square * square)
+    return first, second, freq_x, freq_y, freq_z
+
+
+def elastic_chunk(at, strain_ref, field_ref):
+    elastic = [strain_ref[p, at, :] - field_ref[2 + p, at, :] for p in range(6)]
+    lam, shear2 = field_ref[0, at, :], 2.0 * field_ref[1, at, :]
+    trace = elastic[0] + elastic[1] + elastic[2]
+    stress = [shear2 * e for e in elastic]
+    stress = [stress[p] + lam * trace if p < 3 else stress[p] for p in range(6)]
+    return elastic, trace, stress
+
+
+def elastic_kernel(
+    full_x, full_y, phase_ref, lame_ref, eigen_ref, mz_ref, fx_ref, fy_ref, iy_ref, ix_ref, wz_ref,
+    stress_ref, stored_ref, field_ref, strain_ref, t_ref, *buffers
+):
+    full_z = phase_ref.shape[1]
+    exchanges = 2 * ITERS
+    sent, received = buffers[:exchanges], buffers[exchanges:2 * exchanges]
+    send_sems, recv_sems = buffers[2 * exchanges:3 * exchanges], buffers[3 * exchanges:]
+    greet()
+    chunks = full_z // ROWS
+
+    def fields(step, carry):
+        at = pl.ds(pl.multiple_of(step * ROWS, ROWS), ROWS)
+        phase = [phase_ref[a, at, :] for a in range(4)]
+        for which in range(2):
+            field_ref[which, at, :] = sum(phase[a] * lame_ref[which, a] for a in range(4))
+        for p in range(6):
+            field_ref[2 + p, at, :] = sum(phase[a] * eigen_ref[a, p] for a in range(4))
+            strain_ref[p, at, :] = jnp.zeros_like(phase[0])
+        return carry
+
+    lax.fori_loop(0, chunks, fields, 0)
+    coefs = wave_parts(lame_ref, full_x, full_y, full_z)
+    for turn in range(ITERS):
+        there, back = 2 * turn, 2 * turn + 1
+
+        def stresses(step, carry):
+            at = pl.ds(pl.multiple_of(step * ROWS, ROWS), ROWS)
+            _, _, stress = elastic_chunk(at, strain_ref, field_ref)
+            for p in range(6):
+                t_ref[p, at, :] = stress[p]
+            return carry
+
+        lax.fori_loop(0, chunks, stresses, 0)
+        halves(mz_ref, t_ref, sent[there])
+        exchange_start(sent[there], received[there], send_sems[there], recv_sems[there])
+        exchange_wait(sent[there], received[there], send_sems[there], recv_sems[there], True)
+        plane_green(
+            received[there], sent[back], fx_ref, fy_ref, iy_ref, ix_ref, coefs,
+            full_x, full_y, full_z,
+        )
+        exchange_start(sent[back], received[back], send_sems[back], recv_sems[back])
+        exchange_wait(sent[back], received[back], send_sems[back], recv_sems[back], True)
+        slots = full_z // 2
+        for c in range(6):
+            value = jnp.concatenate([
+                jnp.concatenate([
+                    received[back][pl.ds(c * 4 + r * 2 + h, slots, stride=24), :] for h in range(2)
+                ], axis=1) for r in range(2)
+            ], axis=0)
+            strain_ref[c] = strain_ref[c] - left_product(wz_ref[...], value)
+
+    def finish(step, carry):
+        at = pl.ds(pl.multiple_of(step * ROWS, ROWS), ROWS)
+        elastic, trace, stress = elastic_chunk(at, strain_ref, field_ref)
+        for p in range(6):
+            stress_ref[p, at, :] = stress[p]
+        squares = sum(e * e for e in elastic[:3]) + 2.0 * sum(e * e for e in elastic[3:])
+        for a in range(4):
+            coupling = sum(
+                stress[p] * (eigen_ref[a, p] * (1.0 if p < 3 else 2.0)) for p in range(6)
+            )
+            stored = 0.5 * lame_ref[0, a] * trace * trace + lame_ref[1, a] * squares
+            stored_ref[a, at, :] = stored - coupling
+        return carry
+
+    lax.fori_loop(0, chunks, finish, 0)
+    for t in range(exchanges):
+        exchange_wait(sent[t], received[t], send_sems[t], recv_sems[t], False)
+
+
+def elastic_call(phase, lame, eigen, full_x, full_y):
+    _, size_x, size_y, full_z = phase.shape
+    cells = size_x * size_y
+    count = full_z // 2
+    tables = [jnp.asarray(t) for t in kernel_tables(size_x, full_x, full_y, full_z)]
+    spread = phase.reshape(4, cells, full_z).transpose(0, 2, 1)
+    vmem = pl.BlockSpec(memory_space=pltpu.VMEM)
+    smem = pl.BlockSpec(memory_space=pltpu.SMEM)
+    exchanges = 2 * ITERS
+    big = pltpu.VMEM((count * 24, LANES), jnp.float32)
+    stress, stored = pl.pallas_call(
+        functools.partial(elastic_kernel, full_x, full_y),
+        out_shape=(
+            jax.ShapeDtypeStruct((6, full_z, cells), jnp.float32),
+            jax.ShapeDtypeStruct((4, full_z, cells), jnp.float32),
+        ),
+        in_specs=[vmem, smem, smem] + [vmem] * 6,
+        out_specs=(vmem, vmem),
+        scratch_shapes=[
+            pltpu.VMEM((8, full_z, cells), jnp.float32),
+            pltpu.VMEM((6, full_z, cells), jnp.float32),
+            pltpu.VMEM((6, full_z, cells), jnp.float32),
+        ]
+        + [big] * (2 * exchanges)
+        + [pltpu.SemaphoreType.DMA((count,))] * (2 * exchanges),
+        compiler_params=pltpu.CompilerParams(
+            collective_id=0, has_side_effects=True, vmem_limit_bytes=40 * 1024 * 1024
+        ),
+    )(spread, lame, eigen, *tables)
+    place = lambda x: x.transpose(0, 2, 1).reshape((-1, size_x, size_y, full_z))
+    return place(stress), place(stored)
+
+
 def laplace_padded(padded):
     centre = padded[:, 1:-1, 1:-1, :]
     total = -6.0 * centre
@@ -204,37 +650,34 @@
     full_x = labels.shape[0] * lax.axis_size("gx")
     full_y = labels.shape[1] * lax.axis_size("gy")
     full_z = labels.shape[2]
-    strain = jnp.zeros((6,) + labels.shape, jnp.float32)
-    for _ in range(ITERS):
+    if kernel_fits(labels.shape):
+        stress, stored = elastic_call(phase, lame, eigen, full_x, full_y)
+    else:
+        strain = jnp.zeros((6,) + labels.shape, jnp.float32)
+        step = fluctuation if slots_fit(full_z) else fluctuation_general
+        for _ in range(ITERS):
+            stress = stress_of(strain, eigen_field, lam_field, shear_field)
+            strain = strain - step(stress, full_x, full_y, full_z, lam0, mu0)
         stress = stress_of(strain, eigen_field, lam_field, shear_field)
-        real, imag = spectrum(stress)
-        freq_x, freq_y, freq_z, zero = wave_numbers(real.shape, full_x, full_y, full_z)
-        upd_real = green(real, freq_x, freq_y, freq_z, zero, lam0, mu0)
-        upd_imag = green(imag, freq_x, freq_y, freq_z, zero, lam0, mu0)
-        packed = (upd_real[0::2] - upd_imag[1::2], upd_imag[0::2] + upd_real[1::2])
-        back_real, back_imag = recover(packed)
-        change = jnp.stack([back_real, back_imag], axis=1).reshape(strain.shape)
-        strain = strain - change
-    stress = stress_of(strain, eigen_field, lam_field, shear_field)
+        elastic = strain - eigen_field
+        trace = elastic[0] + elastic[1] + elastic[2]
+        squares = (
+            elastic[0] ** 2
+            + elastic[1] ** 2
+            + elastic[2] ** 2
+            + 2.0 * (elastic[3] ** 2 + elastic[4] ** 2 + elastic[5] ** 2)
+        )
+        weight = jnp.array([1.0, 1.0, 1.0, 2.0, 2.0, 2.0], jnp.float32)
+        coupling = jnp.einsum(
+            "ap,pxyz->axyz", eigen * weight[None], stress, precision=lax.Precision.HIGHEST
+        )
+        stored = (
+            0.5 * (column(lame[0]) * trace[None] ** 2 + 2.0 * column(lame[1]) * squares[None])
+            - coupling
+        )
     deviate = part - column(wells)
     energy = 0.5 * column(curvature) * deviate**2 + 0.25 * column(quartic) * deviate**4
     chemical = energy - chem[None] * part
-    elastic = strain - eigen_field
-    trace = elastic[0] + elastic[1] + elastic[2]
-    squares = (
-        elastic[0] ** 2
-        + elastic[1] ** 2
-        + elastic[2] ** 2
-        + 2.0 * (elastic[3] ** 2 + elastic[4] ** 2 + elastic[5] ** 2)
-    )
-    weight = jnp.array([1.0, 1.0, 1.0, 2.0, 2.0, 2.0], jnp.float32)
-    coupling = jnp.einsum(
-        "ap,pxyz->axyz", eigen * weight[None], stress, precision=lax.Precision.HIGHEST
-    )
-    stored = (
-        0.5 * (column(lame[0]) * trace[None] ** 2 + 2.0 * column(lame[1]) * squares[None])
-        - coupling
-    )
     total_sq = jnp.sum(phase * phase, axis=0)
     barrier = 2.0 * phase * (total_sq[None] - phase * phase)
     laplacian = laplace_padded(padded)

time: 421 us -> 89.3 us (0.21); the launches traced: 413 us -> 89.1 us
  local copies, waits for them, and re-layouts: 168 us -> 3.96 us
  starting transfers between devices: 75.5 us -> 6.99 us
  other arithmetic: 83.2 us -> 16.4 us
  matrix products: 64.3 us -> 0 us
  Pallas kernels: 0 us -> 57.7 us
  waiting for transfers between devices: 17.7 us -> 3.08 us
    all_to_all x16 -> x0, starting transfers between devices: 69.7 us -> none  [the longest x2 11.7 us: spectrum(): lax.all_to_all(real, 'gy', split_axis=3, concat_axis=2, tiled=True)]
    unnamed x193 -> x52, local copies, waits for them, and re-layouts: 70.3 us -> 1.61 us
    dot_general x46 -> x0, matrix products: 64.3 us -> none  [the longest x32 40.5 us: apply_table(): jnp.dot(table, flat, precision=lax.Precision.HIGHEST, preferred_element_t...]
    all_to_all x25 -> x0, local copies, waits for them, and re-layouts: 57.7 us -> none  [the longest x5 9.2 us: spectrum(): lax.all_to_all(imag, 'gy', split_axis=3, concat_axis=2, tiled=True)]
    pallas_call x0 -> x1, Pallas kernels: none -> 57.7 us  [elastic_call(): pl.pallas_call(functools.partial(elastic_kernel, full_x, full_y), out_sha...]
    all_to_all x16 -> x0, other arithmetic: 37 us -> none  [the longest x2 6.67 us: spectrum(): lax.all_to_all(real, 'gy', split_axis=3, concat_axis=2, tiled=True)]
    all_to_all x16 -> x0, waiting for transfers between devices: 17.7 us -> none  [the longest x2 10.3 us: spectrum(): lax.all_to_all(real, 'gy', split_axis=3, concat_axis=2, tiled=True)]
    div x8 -> x0, local copies, waits for them, and re-layouts: 12.6 us -> none  [the longest x4 6.3 us: transform(): (apply_table(cosine, real, axis) - apply_table(sine, imag, axis)) / length]
  transfers between devices with their start and end apart: 20 -> 4, of which waited for: 8 -> 2; matrix products, arithmetic and copies ran while one was open for 41% -> 6% of each run, Pallas kernels for 0% -> 65%
where the time goes in v1:
time: 89.3 us; the launch traced here: 89.1 us
  Pallas kernels  57.7 us (65%)
  other arithmetic  16.4 us (18%)
  starting transfers between devices  6.99 us (8%)
  local copies, waits for them, and re-layouts  3.96 us (4%)
  waiting for transfers between devices  3.08 us (3%)
  between operations  0.92 us (1%)
    pallas_call x1, Pallas kernels, elastic_call(): pl.pallas_call(functools.partial(elastic_kernel, full_x, full_y), out_sha...  57.7 us
    ppermute x2, starting transfers between devices, with_halo(): after = lax.ppermute(initial, axis, down)  6.99 us
    reduce_sum x5, other arithmetic, partition(): jnp.sum(phase * part, axis=0)  5.07 us
    ppermute x2, waiting for transfers between devices, with_halo(): before = lax.ppermute(last, axis, up)  2.71 us
    concatenate x3, other arithmetic, shards(): stacked = jnp.concatenate([phase, chem[None]], axis=0)  2.45 us
    transpose x2, local copies, waits for them, and re-layouts, elastic_call(): place = lambda x: x.transpose(0, 2, 1).reshape((-1, size_x, size_y, full_z))  2.17 us
  transfers between devices with their start and end apart: 4, of which 2 were waited for; matrix products, arithmetic and copies ran while one was open for 6% of the time, Pallas kernels for 65%

profile of v1, /device:TPU:0, one launch (start us, length us, event | category | flops | bytes accessed | tf_op | source)
XLA Modules:
  0.0 89.1 jit_solution(17554750192028014135)
XLA Ops:
  0.6 0.0 copy-start.8
  0.6 1.3 %broadcast_multiply_fusion.1 = (f32[4]{0:T(128)}, f32[4]{0:T(128)S(1)}) fusion(f32[4]{0:T(128)} %param.18), kind=kLoop, calls=%fused_computation.115 | loop fusion | flops 8 | bytes 48 | tf_op jit(solution)/shard_map/mul | solution.py:679
  2.0 0.0 copy-start.18
  2.0 0.0 copy-start.20
  2.0 1.2 %fusion.44 = f32[8,32,64]{2,1,0:T(8,128)S(1)} fusion(f32[4,8,32,64]{3,2,1,0:T(8,128)} %param.15, s32[8,32,64]{2,1,0:T(8,128)} %param.14), kind=kLoop, calls=%fused_computation.118 | loop fusion | flops 245760 | bytes 393216 | tf_op jit(solution)/shard_map/reduce_sum | solution.py:40
  3.2 0.0 copy-done.8
  3.2 0.0 copy-done.9
  3.2 0.0 copy-done.10
  3.2 0.0 copy-done.17
  3.2 0.0 copy-done.18
  3.3 0.0 copy-done.20
  3.3 0.3 fusion.31
  3.5 0.5 multiply_reduce_fusion.4
  4.0 0.1 fusion.50
  4.1 0.7 multiply_reduce_fusion.3
  4.8 0.1 fusion.49
  4.9 1.0 %multiply_reduce_fusion.2 = (f32[8,32,64]{2,1,0:T(8,128)S(1)}, f32[8,32,64]{2,1,0:T(8,128)S(1)}, f32[8,32,64]{2,1,0:T(8,128)S(1)}) fusion(f32[4,8,32,64]{3,2,1,0:T(8,128)S(1)} %get-tuple-element.41, f32[8,32,64]{2,1,0:T(8,128)S(1)} %get-tuple-element.38, f32[8,32,64]{2,1,0:T(8,128)S(1)} %get-tuple-element.37, f32[4]{0:T(128)S(1)} %get-tuple-element.51, ...), kind=kLoop, calls=%fused_computation.88 | loop fusion | flops 3031040 | bytes 1245248 | tf_op jit(solution)/shard_map/reduce_sum | solution.py:55
  5.9 0.1 fusion.48
  6.0 1.2 %multiply_reduce_fusion.1 = (f32[8,32,64]{2,1,0:T(8,128)S(1)}, f32[8,32,64]{2,1,0:T(8,128)S(1)}, f32[8,32,64]{2,1,0:T(8,128)S(1)}, f32[4,8,32,64]{3,2,1,0:T(8,128)S(1)}) fusion(f32[4,8,32,64]{3,2,1,0:T(8,128)S(1)} %get-tuple-element.41, f32[4]{0:T(128)S(1)} %get-tuple-element.51, f32[8,32,64]{2,1,0:T(8,128)S(1)} %get-tuple-element.34, f32[4]{0:T(128)S(1)} %copy-done.17, ...), kind=kLoop, calls=%fused_computation.84 | loop fusion | flops 3883008 | bytes 1638464 | tf_op jit(solution)/shard_map/reduce_sum | solution.py:55
  7.2 0.1 fusion.47
  7.2 0.0 copy-done.22
  7.3 1.6 %multiply_reduce_fusion = (f32[8,32,64]{2,1,0:T(8,128)S(1)}, f32[8,32,64]{2,1,0:T(8,128)S(1)}, f32[8,32,64]{2,1,0:T(8,128)S(1)}, f32[8,32,64]{2,1,0:T(8,128)S(1)}, f32[4,8,32,64]{3,2,1,0:T(8,128)}) fusion(f32[4,8,32,64]{3,2,1,0:T(8,128)S(1)} %get-tuple-element.41, f32[4]{0:T(128)S(1)} %get-tuple-element.51, f32[8,32,64]{2,1,0:T(8,128)S(1)} %get-tuple-element.31, ...), kind=kLoop, calls=%fused_computation.80 | loop fusion | flops 2293760 | bytes 1638464 | tf_op jit(solution)/shard_map/reduce_sum | solution.py:55
  8.9 0.7 fusion.46
  9.6 3.4 %collective-permute-start = (f32[5,1,32,64]{3,2,1,0:T(8,128)S(1)}, f32[5,1,32,64]{3,2,1,0:T(8,128)S(1)}, u32[]{:S(2)}, u32[]{:S(2)}) collective-permute-start(f32[5,1,32,64]{3,2,1,0:T(8,128)S(1)} %get-tuple-element.49), channel_id=1, source_target_pairs={{4,0},{8,4},{12,8},{16,12},{20,16},{24,20},{28,24},{0,28},{5,1},{9... | collective-permute-start | bytes 122888 | tf_op jit(solution)/shard_map/ppermute | solution.py:28
  13.0 0.0 collective-permute-start.1
  13.0 0.6 broadcast_multiply_fusion.3
  13.6 1.1 %fusion.3 = (f32[5,8,32,1]{3,2,1,0:T(8,128)S(1)}, f32[5,8,32,1]{3,2,1,0:T(8,128)}) fusion(f32[4,8,32,64]{3,2,1,0:T(8,128)S(1)} %get-tuple-element.41, f32[1,8,32,64]{3,2,1,0:T(8,128)S(1)} %bitcast.16), kind=kLoop, calls=%fused_computation.29 | loop fusion | flops 2560 | bytes 337920 | tf_op jit(solution)/shard_map/concatenate | solution.py:643
  14.7 0.4 collective-permute-done
  15.0 2.7 %collective-permute-done.1 = f32[5,1,32,64]{3,2,1,0:T(8,128)S(1)} collective-permute-done((f32[5,1,32,64]{3,2,1,0:T(8,128)S(1)}, f32[5,1,32,64]{3,2,1,0:T(8,128)S(1)}, u32[]{:S(2)}, u32[]{:S(2)}) %collective-permute-start.1) | collective-permute-done | bytes 40992 | tf_op jit(solution)/shard_map/ppermute | solution.py:27
  17.7 0.7 pad_maximum_fusion.16
  18.4 0.0 copy-done.16
  18.4 3.6 %collective-permute-start.2 = (f32[5,10,1,64]{3,2,1,0:T(1,128)}, f32[5,10,1,64]{3,2,1,0:T(1,128)S(1)}, u32[]{:S(2)}, u32[]{:S(2)}) collective-permute-start(f32[5,10,1,64]{3,2,1,0:T(1,128)} %get-tuple-element.42), channel_id=1, source_target_pairs={{1,0},{2,1},{3,2},{0,3},{5,4},{6,5},{7,6},{4,7},{9,8},{10,9},{11,1... | collective-permute-start | bytes 38408 | tf_op jit(solution)/shard_map/ppermute | solution.py:28
  22.0 0.0 collective-permute-start.3
  22.0 1.3 %fusion.2 = (f32[5,8,32,63]{3,2,1,0:T(8,128)}, f32[5,8,32,63]{3,2,1,0:T(8,128)}) fusion(f32[4,8,32,64]{3,2,1,0:T(8,128)S(1)} %get-tuple-element.41, f32[1,8,32,64]{3,2,1,0:T(8,128)S(1)} %bitcast.18), kind=kLoop, calls=%fused_computation.28 | loop fusion | flops 161280 | bytes 972800 | tf_op jit(solution)/shard_map/concatenate | solution.py:643
  23.4 0.0 copy-start.4
  23.4 0.0 copy-start.5
  23.4 0.2 copy.20
  23.6 0.0 copy-start.7
  23.6 0.0 copy-done.6
  23.6 0.7 copy-done
  24.3 0.1 copy-done.1
  24.4 0.0 copy-done.2
  24.4 0.0 copy-done.3
  24.4 57.7 %shard_map.157 = (f32[6,64,256]{2,1,0:T(8,128)S(1)}, f32[4,64,256]{2,1,0:T(8,128)S(1)}) custom-call(f32[4,64,256]{2,1,0:T(8,128)S(1)} %bitcast.11, f32[2,4]{1,0:T(2,128)S(1)} %copy-done.7, f32[4,6]{1,0:T(4,128)S(1)} %copy-done.6, bf16[64,192]{1,0:T(8,128)(2,1)S(1)} %copy-done.4, bf16[128,384]{1,0:T(8,128)(2,1)S(1)} %copy-done.2, ...), custom_call_target="tpu_custom_call" | custom-call | tf_op jit(solution)/shard_map/pallas_call | solution.py:608
  82.1 0.0 copy-start.12
  82.1 1.0 %copy.21 = f32[4,256,64]{2,1,0:T(8,128)} copy(f32[4,256,64]{1,2,0:T(8,128)S(1)} %bitcast.13) | data formatting | bytes 524288 | tf_op jit(solution)/shard_map/transpose | solution.py:627
  83.1 1.2 %copy.22 = f32[6,256,64]{2,1,0:T(8,128)} copy(f32[6,256,64]{1,2,0:T(8,128)S(1)} %bitcast.12) | data formatting | bytes 786432 | tf_op jit(solution)/shard_map/transpose | solution.py:627
  84.3 0.0 collective-permute-done.2
  84.3 0.0 collective-permute-done.3
  84.3 0.0 copy-done.11
  84.3 0.0 copy-start.13
  84.3 0.0 copy-start.14
  84.3 1.8 %fusion.10 = f32[5,8,32,64]{3,2,1,0:T(8,128)S(1)} fusion(f32[1,8,32,64]{3,2,1,0:T(8,128)S(1)} %bitcast.19, f32[4,8,32,64]{3,2,1,0:T(8,128)S(1)} %get-tuple-element.41, f32[5,10,1,64]{3,2,1,0:T(1,128)} %collective-permute-done.3, f32[5,1,32,64]{3,2,1,0:T(8,128)S(1)} %collective-permute-done, f32[5,1,32,64]{3,2,1,0:T(8,128)} %copy-done.16, ...), kind=kLoop, calls=%fused_computation.36 | loop fusion | flops 1802240 | bytes 1418240 | tf_op jit(solution)/shard_map/add | solution.py:636
  86.1 0.0 copy-start.15
  86.1 0.0 copy-start.24
  86.1 0.0 copy-start.25
  86.1 0.7 fusion.41
  86.8 0.2 copy-done.15
  87.0 0.0 copy-done.25
  87.0 0.5 copy-done.19
  87.5 0.0 copy-done.21
  87.5 0.0 copy-done.23
  87.5 0.6 fusion.45
  88.1 0.9 %multiply_subtract_fusion = f32[4,8,32,64]{3,2,1,0:T(8,128)} fusion(f32[4,8,32,64]{3,2,1,0:T(8,128)S(1)} %get-tuple-element.41, f32[4,8,32,64]{3,2,1,0:T(8,128)S(1)} %get-tuple-element.27, f32[8,32,64]{2,1,0:T(8,128)S(1)} %broadcast_multiply_fusion), kind=kLoop, calls=%fused_computation.77 | loop fusion | flops 196608 | bytes 851968 | tf_op jit(solution)/shard_map/sub | solution.py:685
  (23 shorter events, 0.1 us)
Async XLA Ops:
  0.6 2.6 %copy-start.8 = (f32[4,8,32,64]{3,2,1,0:T(8,128)S(1)}, f32[4,8,32,64]{3,2,1,0:T(8,128)}, u32[]{:S(2)}) copy-start(f32[4,8,32,64]{3,2,1,0:T(8,128)} %param.15) | copy-start | bytes 786436
  1.9 5.3 %copy-start.22 = (f32[4]{0:T(128)}, f32[4]{0:T(128)S(1)}, u32[]{:S(2)}) copy-start(f32[4]{0:T(128)S(1)} %get-tuple-element.51) | copy-start | bytes 52
  1.9 1.3 %copy-start.9 = (f32[8,32,64]{2,1,0:T(8,128)S(1)}, f32[8,32,64]{2,1,0:T(8,128)}, u32[]{:S(2)}) copy-start(f32[8,32,64]{2,1,0:T(8,128)} %param.16) | copy-start | bytes 196612
  1.9 1.3 %copy-start.10 = (s32[8,32,64]{2,1,0:T(8,128)S(1)}, s32[8,32,64]{2,1,0:T(8,128)}, u32[]{:S(2)}) copy-start(s32[8,32,64]{2,1,0:T(8,128)} %param.14) | copy-start | bytes 196612
  2.0 1.3 %copy-start.17 = (f32[4]{0:T(128)S(1)}, f32[4]{0:T(128)}, u32[]{:S(2)}) copy-start(f32[4]{0:T(128)} %param.18) | copy-start | bytes 52
  2.0 1.3 %copy-start.18 = (f32[4]{0:T(128)S(1)}, f32[4]{0:T(128)}, u32[]{:S(2)}) copy-start(f32[4]{0:T(128)} %param.19) | copy-start | bytes 52
  2.0 1.3 %copy-start.20 = (f32[4]{0:T(128)S(1)}, f32[4]{0:T(128)}, u32[]{:S(2)}) copy-start(f32[4]{0:T(128)} %param.17) | copy-start | bytes 52
  9.6 5.4 %collective-permute-start = (f32[5,1,32,64]{3,2,1,0:T(8,128)S(1)}, f32[5,1,32,64]{3,2,1,0:T(8,128)S(1)}, u32[]{:S(2)}, u32[]{:S(2)}) collective-permute-start(f32[5,1,32,64]{3,2,1,0:T(8,128)S(1)} %get-tuple-element.49), channel_id=1, source_target_pairs={{4,0},{8,4},{12,8},{16,12},{20,16},{24,20},{28,24},{0,28},{5,1},{9... | collective-permute-start | bytes 122888 | tf_op jit(solution)/shard_map/ppermute | solution.py:28
  13.0 4.8 %collective-permute-start.1 = (f32[5,1,32,64]{3,2,1,0:T(8,128)S(1)}, f32[5,1,32,64]{3,2,1,0:T(8,128)S(1)}, u32[]{:S(2)}, u32[]{:S(2)}) collective-permute-start(f32[5,1,32,64]{3,2,1,0:T(8,128)S(1)} %get-tuple-element.48), channel_id=1, source_target_pairs={{0,4},{4,8},{8,12},{12,16},{16,20},{20,24},{24,28},{28,0},{1,5},{5... | collective-permute-start | bytes 122888 | tf_op jit(solution)/shard_map/ppermute | solution.py:27
  17.7 0.7 copy-start.16
  18.4 65.9 %collective-permute-start.2 = (f32[5,10,1,64]{3,2,1,0:T(1,128)}, f32[5,10,1,64]{3,2,1,0:T(1,128)S(1)}, u32[]{:S(2)}, u32[]{:S(2)}) collective-permute-start(f32[5,10,1,64]{3,2,1,0:T(1,128)} %get-tuple-element.42), channel_id=1, source_target_pairs={{1,0},{2,1},{3,2},{0,3},{5,4},{6,5},{7,6},{4,7},{9,8},{10,9},{11,1... | collective-permute-start | bytes 38408 | tf_op jit(solution)/shard_map/ppermute | solution.py:28
  22.0 62.3 %collective-permute-start.3 = (f32[5,10,1,64]{3,2,1,0:T(1,128)}, f32[5,10,1,64]{3,2,1,0:T(1,128)}, u32[]{:S(2)}, u32[]{:S(2)}) collective-permute-start(f32[5,10,1,64]{3,2,1,0:T(1,128)} %get-tuple-element.43), channel_id=1, source_target_pairs={{0,1},{1,2},{2,3},{3,0},{4,5},{5,6},{6,7},{7,4},{8,9},{9,10},{10,1... | collective-permute-start | bytes 38408 | tf_op jit(solution)/shard_map/ppermute | solution.py:27
  22.0 1.6 %copy-start.6 = (f32[4,6]{1,0:T(4,128)S(1)}, f32[4,6]{1,0:T(4,128)}, u32[]{:S(2)}) copy-start(f32[4,6]{1,0:T(4,128)} %eigen_ref.1) | copy-start | bytes 292
  23.3 1.0 %copy-start = (bf16[2,256,256]{2,1,0:T(8,128)(2,1)S(1)}, bf16[2,256,256]{2,1,0:T(8,128)(2,1)}, u32[]{:S(2)}) copy-start(bf16[2,256,256]{2,1,0:T(8,128)(2,1)} %constant.33.clone.fy_ref) | copy-start | bytes 786436
  23.3 1.0 %copy-start.1 = (bf16[2,256,256]{2,1,0:T(8,128)(2,1)S(1)}, bf16[2,256,256]{2,1,0:T(8,128)(2,1)}, u32[]{:S(2)}) copy-start(bf16[2,256,256]{2,1,0:T(8,128)(2,1)} %constant.34.clone.iy_ref) | copy-start | bytes 786436
  23.3 1.0 %copy-start.2 = (bf16[128,384]{1,0:T(8,128)(2,1)S(1)}, bf16[128,384]{1,0:T(8,128)(2,1)}, u32[]{:S(2)}) copy-start(bf16[128,384]{1,0:T(8,128)(2,1)} %constant.32.clone.fx_ref) | copy-start | bytes 294916
  23.3 1.1 %copy-start.3 = (bf16[128,384]{1,0:T(8,128)(2,1)S(1)}, bf16[128,384]{1,0:T(8,128)(2,1)}, u32[]{:S(2)}) copy-start(bf16[128,384]{1,0:T(8,128)(2,1)} %constant.35.clone.ix_ref) | copy-start | bytes 294916
  23.4 1.1 %copy-start.4 = (bf16[64,192]{1,0:T(8,128)(2,1)S(1)}, bf16[64,192]{1,0:T(8,128)(2,1)}, u32[]{:S(2)}) copy-start(bf16[64,192]{1,0:T(8,128)(2,1)} %constant.31.clone.mz_ref) | copy-start | bytes 73732
  23.4 1.1 %copy-start.5 = (bf16[64,192]{1,0:T(8,128)(2,1)S(1)}, bf16[64,192]{1,0:T(8,128)(2,1)}, u32[]{:S(2)}) copy-start(bf16[64,192]{1,0:T(8,128)(2,1)} %constant.36.clone.wz_ref) | copy-start | bytes 73732
  23.6 0.9 copy-start.7
  82.1 2.2 %copy-start.12 = (f32[5,8,32,63]{3,2,1,0:T(8,128)S(1)}, f32[5,8,32,63]{3,2,1,0:T(8,128)}, u32[]{:S(2)}) copy-start(f32[5,8,32,63]{3,2,1,0:T(8,128)} %get-tuple-element.44) | copy-start | bytes 967684
  83.1 1.2 %copy-start.11 = (f32[5,8,32,1]{3,2,1,0:T(8,128)S(1)}, f32[5,8,32,1]{3,2,1,0:T(8,128)}, u32[]{:S(2)}) copy-start(f32[5,8,32,1]{3,2,1,0:T(8,128)} %get-tuple-element.47) | copy-start | bytes 15364
  84.3 2.5 %copy-start.13 = (f32[4,256,64]{2,1,0:T(8,128)S(1)}, f32[4,256,64]{2,1,0:T(8,128)}, u32[]{:S(2)}) copy-start(f32[4,256,64]{2,1,0:T(8,128)} %copy.21) | copy-start | bytes 786436
  84.3 2.5 %copy-start.14 = (f32[4,8,32,64]{3,2,1,0:T(8,128)S(1)}, f32[4,8,32,64]{3,2,1,0:T(8,128)}, u32[]{:S(2)}) copy-start(f32[4,8,32,64]{3,2,1,0:T(8,128)} %get-tuple-element.30) | copy-start | bytes 786436
  86.1 0.9 %copy-start.15 = (f32[8,32,64]{2,1,0:T(8,128)S(1)}, f32[8,32,64]{2,1,0:T(8,128)}, u32[]{:S(2)}) copy-start(f32[8,32,64]{2,1,0:T(8,128)} %get-tuple-element.29) | copy-start | bytes 196612
  86.1 0.9 %copy-start.24 = (f32[4]{0:T(128)S(1)}, f32[4]{0:T(128)}, u32[]{:S(2)}) copy-start(f32[4]{0:T(128)} %get-tuple-element.50) | copy-start | bytes 52
  86.1 0.9 copy-start.25
  86.8 0.7 copy-start.19
  86.8 0.7 copy-start.21
  86.8 0.7 copy-start.23

commit v2 on v1

--- a/solution.py
+++ b/solution.py
@@ -354,10 +354,15 @@
         return carry
 
     lax.fori_loop(1, count, hello, 0)
-    pl.semaphore_wait(barrier, count - 1)
-
-
-def exchange_copy(sent, received, send_sem, recv_sem, source, target):
+
+
+def greeted():
+    count = lax.axis_size("gx") * lax.axis_size("gy")
+    pl.semaphore_wait(pltpu.get_barrier_semaphore(), count - 1)
+
+
+def exchange_copy(pack, source, target):
+    sent, received, send_sem, recv_sem = pack
     rows = sent.shape[0] // (lax.axis_size("gx") * lax.axis_size("gy"))
     return pltpu.make_async_remote_copy(
         src_ref=sent.at[pl.ds(pl.multiple_of(target * rows, 8), rows)],
@@ -369,14 +374,14 @@
     )
 
 
-def exchange_start(sent, received, send_sem, recv_sem):
+def exchange_start(pack):
+    sent, received = pack[:2]
     count = lax.axis_size("gx") * lax.axis_size("gy")
     me = position()
     rows = sent.shape[0] // count
 
     def send(step, carry):
-        target = lax.rem(me + step, count)
-        exchange_copy(sent, received, send_sem, recv_sem, me, target).start()
+        exchange_copy(pack, me, lax.rem(me + step, count)).start()
         return carry
 
     lax.fori_loop(1, count, send, 0)
@@ -384,16 +389,16 @@
     received[own, :] = sent[own, :]
 
 
-def exchange_wait(sent, received, send_sem, recv_sem, arrived):
+def exchange_wait(pack, arrived):
     count = lax.axis_size("gx") * lax.axis_size("gy")
     me = position()
 
     def wait(step, carry):
         other = lax.rem(me + step, count)
         if arrived:
-            exchange_copy(sent, received, send_sem, recv_sem, other, other).wait_recv()
+            exchange_copy(pack, other, other).wait_recv()
         else:
-            exchange_copy(sent, received, send_sem, recv_sem, me, other).wait_send()
+            exchange_copy(pack, me, other).wait_send()
         return carry
 
     lax.fori_loop(1, count, wait, 0)
@@ -414,19 +419,22 @@
     return result
 
 
-def halves(z_ref, t_ref, sent):
+GROUPS = ((0, 4), (4, 6))
+
+
+def halves(z_ref, t_ref, sent, group):
     slots = z_ref.shape[0] // 2
-    rows = 4 * 6
-    for c in range(6):
+    rows = 4 * (group[1] - group[0])
+    for c in range(*group):
         result = left_product(z_ref[...], t_ref[c])
         for r in range(2):
             for h in range(2):
                 piece = result[r * slots:(r + 1) * slots, h * LANES:(h + 1) * LANES]
-                sent[pl.ds(c * 4 + r * 2 + h, slots, stride=rows), :] = piece
-
-
-def plane_rows(received, c, r, count_y):
-    rows = 4 * 6
+                first = (c - group[0]) * 4 + r * 2 + h
+                sent[pl.ds(first, slots, stride=rows), :] = piece
+
+
+def plane_rows(received, c, r, count_y, rows):
     result = []
     for h in range(2):
         first = c * 4 + r * 2 + h
@@ -438,8 +446,7 @@
     return jnp.concatenate(result, axis=0)
 
 
-def plane_store(sent, value, c, r, count_y):
-    rows = 4 * 6
+def plane_store(sent, value, c, r, count_y, rows):
     for h in range(2):
         first = c * 4 + r * 2 + h
         parts = [
@@ -449,43 +456,76 @@
             sent[pl.ds(j * rows + first, ROWS, stride=rows * count_y), :] = part
 
 
-def plane_green(received, sent, fx_ref, fy_ref, iy_ref, ix_ref, coefs, full_x, full_y, full_z):
+def plane_forward(received, plane_ref, fx_ref, fy_ref, group, full_x, full_y):
     count_y = lax.axis_size("gy")
+    number = group[1] - group[0]
     rows_x = []
-    for c in range(6):
-        both = [plane_rows(received, c, r, count_y) for r in range(2)]
+    for c in range(number):
+        both = [plane_rows(received, c, r, count_y, 4 * number) for r in range(2)]
         rows_x.append(jnp.concatenate(both, axis=0))
     spec = left_product(fx_ref[...], jnp.concatenate(rows_x, axis=1))
     lanes = []
-    for c in range(6):
+    for c in range(number):
         part = spec[:, c * full_y:(c + 1) * full_y]
         lanes.append(jnp.concatenate([part[:full_x], part[full_x:]], axis=1))
     spec = right_product(jnp.concatenate(lanes, axis=0), fy_ref)
-    first, second, freq_x, freq_y, freq_z = coefs
-    tau = [spec[c * full_x:(c + 1) * full_x] for c in range(6)]
-    vec_x = tau[0] * freq_x + tau[5] * freq_y + tau[4] * freq_z
-    vec_y = tau[5] * freq_x + tau[1] * freq_y + tau[3] * freq_z
-    vec_z = tau[4] * freq_x + tau[3] * freq_y + tau[2] * freq_z
-    inner = (freq_x * vec_x + freq_y * vec_y + freq_z * vec_z) * second
-    pairs = (
-        (freq_x, vec_x, freq_x, vec_x),
-        (freq_y, vec_y, freq_y, vec_y),
-        (freq_z, vec_z, freq_z, vec_z),
-        (freq_y, vec_y, freq_z, vec_z),
-        (freq_x, vec_x, freq_z, vec_z),
-        (freq_x, vec_x, freq_y, vec_y),
-    )
-    spec = [(fk * vh + fh * vk) * first - fk * fh * inner for fk, vk, fh, vh in pairs]
-    spec = right_product(jnp.concatenate(spec, axis=0), iy_ref)
+    plane_ref[group[0] * full_x:group[1] * full_x, :] = spec
+
+
+def plane_green(plane_ref, wave_ref, full_x, full_z):
+    freq_z = lax.convert_element_type(position(), jnp.float32) * (1.0 / full_z)
+
+    def chunk(step, carry):
+        start = pl.multiple_of(step * ROWS, ROWS)
+        at = pl.ds(start, ROWS)
+        where = [pl.ds(pl.multiple_of(c * full_x + start, ROWS), ROWS) for c in range(6)]
+        first, second, freq_x, freq_y = [wave_ref[w, at, :] for w in range(4)]
+        tau = [plane_ref[where[c], :] for c in range(6)]
+        vec_x = tau[0] * freq_x + tau[5] * freq_y + tau[4] * freq_z
+        vec_y = tau[5] * freq_x + tau[1] * freq_y + tau[3] * freq_z
+        vec_z = tau[4] * freq_x + tau[3] * freq_y + tau[2] * freq_z
+        inner = (freq_x * vec_x + freq_y * vec_y + freq_z * vec_z) * second
+        pairs = (
+            (freq_x, vec_x, freq_x, vec_x),
+            (freq_y, vec_y, freq_y, vec_y),
+            (freq_z, vec_z, freq_z, vec_z),
+            (freq_y, vec_y, freq_z, vec_z),
+            (freq_x, vec_x, freq_z, vec_z),
+            (freq_x, vec_x, freq_y, vec_y),
+        )
+        for c, (fk, vk, fh, vh) in enumerate(pairs):
+            plane_ref[where[c], :] = (fk * vh + fh * vk) * first - fk * fh * inner
+        return carry
+
+    lax.fori_loop(0, full_x // ROWS, chunk, 0)
+
+
+def plane_back(plane_ref, sent, iy_ref, ix_ref, group, full_x, full_y):
+    count_y = lax.axis_size("gy")
+    number = group[1] - group[0]
+    spec = right_product(plane_ref[group[0] * full_x:group[1] * full_x, :], iy_ref)
     lanes = []
-    for c in range(6):
+    for c in range(number):
         part = spec[c * full_x:(c + 1) * full_x]
         lanes.append(jnp.concatenate([part[:, :full_y], part[:, full_y:]], axis=0))
     plane = left_product(ix_ref[...], jnp.concatenate(lanes, axis=1))
-    for c in range(6):
+    for c in range(number):
         for r in range(2):
             value = plane[r * full_x:(r + 1) * full_x, c * full_y:(c + 1) * full_y]
-            plane_store(sent, value, c, r, count_y)
+            plane_store(sent, value, c, r, count_y, 4 * number)
+
+
+def strain_update(received, wz_ref, strain_ref, group):
+    slots = wz_ref.shape[0] // 2
+    rows = 4 * (group[1] - group[0])
+    for c in range(*group):
+        value = jnp.concatenate([
+            jnp.concatenate([
+                received[pl.ds((c - group[0]) * 4 + r * 2 + h, slots, stride=rows), :]
+                for h in range(2)
+            ], axis=1) for r in range(2)
+        ], axis=0)
+        strain_ref[c] = strain_ref[c] - left_product(wz_ref[...], value)
 
 
 def wave_parts(lame_ref, full_x, full_y, full_z):
@@ -524,108 +564,303 @@
     return elastic, trace, stress
 
 
-def elastic_kernel(
-    full_x, full_y, phase_ref, lame_ref, eigen_ref, mz_ref, fx_ref, fy_ref, iy_ref, ix_ref, wz_ref,
-    stress_ref, stored_ref, field_ref, strain_ref, t_ref, *buffers
+def half(h):
+    return slice(h * LANES, (h + 1) * LANES)
+
+
+def turned(value, shift):
+    shift = shift % LANES
+    return pltpu.roll(value, shift, 1) if shift else value
+
+
+def lane_block(shape, width):
+    return lax.broadcasted_iota(jnp.int32, shape, 1) // width
+
+
+def lane_place(shape, width):
+    return lax.broadcasted_iota(jnp.int32, shape, 1) % width
+
+
+def halo_pack(phase_ref, chem_ref, x_up, x_down, y_up, y_down, width):
+    full_z = phase_ref.shape[1]
+    blocks = LANES // width
+    fold = full_z // blocks
+    block = lane_block((full_z, LANES), width)
+    place = lane_place((full_z, LANES), width)
+    fields = [phase_ref[f] for f in range(4)] + [chem_ref[...]]
+    for face, h, own in ((x_up, 1, blocks - 1), (x_down, 0, 0)):
+        total = turned(fields[0][:, half(h)], -width * own)
+        for f in range(1, 4):
+            total = jnp.where(block == f, turned(fields[f][:, half(h)], width * (f - own)), total)
+        face[:full_z, :] = total
+        parts = [fields[4][k * fold:(k + 1) * fold, half(h)] for k in range(blocks)]
+        total = turned(parts[0], -width * own)
+        for k in range(1, blocks):
+            total = jnp.where(block[:fold] == k, turned(parts[k], width * (k - own)), total)
+        face[full_z:, :] = total
+    for face, own in ((y_up, width - 1), (y_down, 0)):
+        total = jnp.zeros((full_z, LANES), jnp.float32)
+        for f in range(5):
+            for h in range(2):
+                slot = 8 * h + f
+                total = jnp.where(place == slot, turned(fields[f][:, half(h)], slot - own), total)
+        face[...] = total
+
+
+def halo_laplace(f, field, x_before, x_after, y_before, y_after, width):
+    full_z = field.shape[0]
+    blocks = LANES // width
+    fold = full_z // blocks
+    block = lane_block((full_z, LANES), width)
+    place = lane_place((full_z, LANES), width)
+
+    def face(ref, own):
+        if f < 4:
+            return turned(ref[:full_z, :], width * (own - f))
+        folded = ref[full_z:, :]
+        return jnp.concatenate([turned(folded, width * (own - k)) for k in range(blocks)], axis=0)
+
+    sides = [field[:, half(h)] for h in range(2)]
+    right = [turned(side, width) for side in sides]
+    left = [turned(side, -width) for side in sides]
+    last = blocks - 1
+    result = []
+    for h in range(2):
+        slot = 8 * h + f
+        side = sides[h]
+        below = jnp.where(block == 0, face(x_before, 0) if h == 0 else right[0], right[h])
+        above = jnp.where(block == last, left[1] if h == 0 else face(x_after, last), left[h])
+        total = below + above - 6.0 * side
+        total += jnp.where(place == 0, turned(y_before[...], -slot), turned(side, 1))
+        after = turned(y_after[...], width - 1 - slot)
+        total += jnp.where(place == width - 1, after, turned(side, -1))
+        total += pltpu.roll(side, 1, 0) + pltpu.roll(side, full_z - 1, 0)
+        result.append(total)
+    return result
+
+
+def newton_chunk(phase, conc, scalars):
+    curve, quart, wells = scalars
+    part = [conc for _ in range(4)]
+    dev = [conc - wells[a] for a in range(4)]
+    chem = sum(
+        phase[a] * (curve[a] * dev[a] + quart[a] * (dev[a] * dev[a] * dev[a])) for a in range(4)
+    )
+    for _ in range(NEWTON):
+        dev = [part[a] - wells[a] for a in range(4)]
+        square = [d * d for d in dev]
+        slope = [dev[a] * (curve[a] + quart[a] * square[a]) - chem for a in range(4)]
+        soft = [1.0 / (curve[a] + (3.0 * quart[a]) * square[a]) for a in range(4)]
+        weight = [phase[a] * soft[a] for a in range(4)]
+        top = conc - sum(phase[a] * part[a] for a in range(4))
+        top = top + sum(weight[a] * slope[a] for a in range(4))
+        shift = top / sum(weight)
+        part = [part[a] + (shift - slope[a]) * soft[a] for a in range(4)]
+        chem = chem + shift
+    dev = [part[a] - wells[a] for a in range(4)]
+    square = [d * d for d in dev]
+    total = sum(p * p for p in phase)
+    local = []
+    for a in range(4):
+        energy = square[a] * (0.5 * curve[a] + (0.25 * quart[a]) * square[a])
+        barrier = 2.0 * phase[a] * (total - phase[a] * phase[a])
+        local.append(energy - chem * part[a] + barrier)
+    return chem, local
+
+
+def step_kernel(
+    full_x, full_y, labels_ref, noise_ref, raw_conc_ref, curve_ref, quart_ref, wells_ref, lame_ref,
+    eigen_ref, mz_ref, fx_ref, fy_ref, iy_ref, ix_ref, wz_ref,
+    next_ref, conc_next_ref, stress_ref,
+    phase_ref, conc_ref, chem_ref, local_ref, field_ref, strain_ref, t_ref, plane_ref, wave_ref,
+    *buffers
 ):
     full_z = phase_ref.shape[1]
-    exchanges = 2 * ITERS
-    sent, received = buffers[:exchanges], buffers[exchanges:2 * exchanges]
-    send_sems, recv_sems = buffers[2 * exchanges:3 * exchanges], buffers[3 * exchanges:]
+    chunks = full_z // ROWS
+    width = full_y // lax.axis_size("gy")
+    number = 2 * ITERS * len(GROUPS)
+    packs = [buffers[4 * n:4 * n + 4] for n in range(number)]
+    packs = [packs[n:n + len(GROUPS)] for n in range(0, number, len(GROUPS))]
+    halo_sent, halo_got = buffers[4 * number:4 * number + 4], buffers[4 * number + 4:4 * number + 8]
+    halo_send, halo_recv = buffers[4 * number + 8:]
     greet()
-    chunks = full_z // ROWS
+
+    for h in range(2):
+        at = pl.ds(h * LANES, LANES)
+        label = labels_ref[at, :]
+        raw = [noise_ref[a, at, :] + jnp.where(label == a, 2.0, 0.0) for a in range(4)]
+        total = raw[0] + raw[1] + raw[2] + raw[3]
+        for a in range(4):
+            phase_ref[a, :, half(h)] = (raw[a] / total).T
+        conc_ref[:, half(h)] = raw_conc_ref[at, :].T
+
+    def rows_at(step):
+        return pl.ds(pl.multiple_of(step * ROWS, ROWS), ROWS)
 
     def fields(step, carry):
-        at = pl.ds(pl.multiple_of(step * ROWS, ROWS), ROWS)
+        at = rows_at(step)
         phase = [phase_ref[a, at, :] for a in range(4)]
         for which in range(2):
             field_ref[which, at, :] = sum(phase[a] * lame_ref[which, a] for a in range(4))
         for p in range(6):
             field_ref[2 + p, at, :] = sum(phase[a] * eigen_ref[a, p] for a in range(4))
             strain_ref[p, at, :] = jnp.zeros_like(phase[0])
+        _, _, stress = elastic_chunk(at, strain_ref, field_ref)
+        for p in range(6):
+            t_ref[p, at, :] = stress[p]
         return carry
 
-    lax.fori_loop(0, chunks, fields, 0)
-    coefs = wave_parts(lame_ref, full_x, full_y, full_z)
+    def stresses(step, carry):
+        at = rows_at(step)
+        _, _, stress = elastic_chunk(at, strain_ref, field_ref)
+        for p in range(6):
+            t_ref[p, at, :] = stress[p]
+        return carry
+
+    def newton(step, carry):
+        at = rows_at(step)
+        phase = [phase_ref[a, at, :] for a in range(4)]
+        scalars = [[ref[a] for a in range(4)] for ref in (curve_ref, quart_ref, wells_ref)]
+        chem, local = newton_chunk(phase, conc_ref[at, :], scalars)
+        chem_ref[at, :] = chem
+        for a in range(4):
+            local_ref[a, at, :] = local[a]
+        return carry
+
+    def halo_copies():
+        i, j = lax.axis_index("gx"), lax.axis_index("gy")
+        count_x, count_y = lax.axis_size("gx"), lax.axis_size("gy")
+        targets = (
+            (lax.rem(i + 1, count_x), j),
+            (lax.rem(i + count_x - 1, count_x), j),
+            (i, lax.rem(j + 1, count_y)),
+            (i, lax.rem(j + count_y - 1, count_y)),
+        )
+        return [
+            pltpu.make_async_remote_copy(
+                src_ref=halo_sent[n],
+                dst_ref=halo_got[n],
+                send_sem=halo_send.at[n],
+                recv_sem=halo_recv.at[n],
+                device_id=target,
+                device_id_type=MESH,
+            )
+            for n, target in enumerate(targets)
+        ]
+
+    def beside_first():
+        for w, value in enumerate(wave_parts(lame_ref, full_x, full_y, full_z)[:4]):
+            wave_ref[w] = value
+        lax.fori_loop(0, chunks, newton, 0)
+        halo_pack(phase_ref, chem_ref, *halo_sent, width)
+        for copy in halo_copies():
+            copy.start()
+
+    def beside_second():
+        for copy in halo_copies():
+            copy.wait_recv()
+        for f in range(5):
+            field = phase_ref[f] if f < 4 else chem_ref[...]
+            spread = halo_laplace(f, field, *halo_got, width)
+            for h in range(2):
+                if f < 4:
+                    local_ref[f, :, half(h)] = local_ref[f, :, half(h)] - spread[h]
+                else:
+                    conc_next_ref[:, half(h)] = conc_ref[:, half(h)] + step_conc * spread[h]
+
     for turn in range(ITERS):
-        there, back = 2 * turn, 2 * turn + 1
-
-        def stresses(step, carry):
-            at = pl.ds(pl.multiple_of(step * ROWS, ROWS), ROWS)
-            _, _, stress = elastic_chunk(at, strain_ref, field_ref)
-            for p in range(6):
-                t_ref[p, at, :] = stress[p]
-            return carry
-
-        lax.fori_loop(0, chunks, stresses, 0)
-        halves(mz_ref, t_ref, sent[there])
-        exchange_start(sent[there], received[there], send_sems[there], recv_sems[there])
-        exchange_wait(sent[there], received[there], send_sems[there], recv_sems[there], True)
-        plane_green(
-            received[there], sent[back], fx_ref, fy_ref, iy_ref, ix_ref, coefs,
-            full_x, full_y, full_z,
-        )
-        exchange_start(sent[back], received[back], send_sems[back], recv_sems[back])
-        exchange_wait(sent[back], received[back], send_sems[back], recv_sems[back], True)
-        slots = full_z // 2
-        for c in range(6):
-            value = jnp.concatenate([
-                jnp.concatenate([
-                    received[back][pl.ds(c * 4 + r * 2 + h, slots, stride=24), :] for h in range(2)
-                ], axis=1) for r in range(2)
-            ], axis=0)
-            strain_ref[c] = strain_ref[c] - left_product(wz_ref[...], value)
+        there, back = packs[2 * turn], packs[2 * turn + 1]
+        lax.fori_loop(0, chunks, stresses if turn else fields, 0)
+        for pack, group in zip(there, GROUPS):
+            halves(mz_ref, t_ref, pack[0], group)
+            if turn == 0 and group is GROUPS[0]:
+                greeted()
+            exchange_start(pack)
+        if turn == 0:
+            beside_first()
+        for pack, group in zip(there, GROUPS):
+            exchange_wait(pack, True)
+            plane_forward(pack[1], plane_ref, fx_ref, fy_ref, group, full_x, full_y)
+        plane_green(plane_ref, wave_ref, full_x, full_z)
+        for pack, group in zip(back, GROUPS):
+            plane_back(plane_ref, pack[0], iy_ref, ix_ref, group, full_x, full_y)
+            exchange_start(pack)
+        if turn == 0:
+            beside_second()
+        for pack, group in zip(back, GROUPS):
+            exchange_wait(pack, True)
+            strain_update(pack[1], wz_ref, strain_ref, group)
 
     def finish(step, carry):
-        at = pl.ds(pl.multiple_of(step * ROWS, ROWS), ROWS)
+        at = rows_at(step)
         elastic, trace, stress = elastic_chunk(at, strain_ref, field_ref)
         for p in range(6):
             stress_ref[p, at, :] = stress[p]
         squares = sum(e * e for e in elastic[:3]) + 2.0 * sum(e * e for e in elastic[3:])
+        force = []
         for a in range(4):
             coupling = sum(
                 stress[p] * (eigen_ref[a, p] * (1.0 if p < 3 else 2.0)) for p in range(6)
             )
             stored = 0.5 * lame_ref[0, a] * trace * trace + lame_ref[1, a] * squares
-            stored_ref[a, at, :] = stored - coupling
+            force.append(local_ref[a, at, :] + (stored - coupling))
+        mean = 0.25 * (force[0] + force[1] + force[2] + force[3])
+        for a in range(4):
+            next_ref[a, at, :] = phase_ref[a, at, :] - step_phase * (force[a] - mean)
         return carry
 
     lax.fori_loop(0, chunks, finish, 0)
-    for t in range(exchanges):
-        exchange_wait(sent[t], received[t], send_sems[t], recv_sems[t], False)
-
-
-def elastic_call(phase, lame, eigen, full_x, full_y):
-    _, size_x, size_y, full_z = phase.shape
+    for group_packs in packs:
+        for pack in group_packs:
+            exchange_wait(pack, False)
+    for copy in halo_copies():
+        copy.wait_send()
+
+
+def step_call(labels, seed_noise, conc, curvature, quartic, wells, lame, eigen, full_x, full_y):
+    size_x, size_y, full_z = labels.shape
     cells = size_x * size_y
     count = full_z // 2
     tables = [jnp.asarray(t) for t in kernel_tables(size_x, full_x, full_y, full_z)]
-    spread = phase.reshape(4, cells, full_z).transpose(0, 2, 1)
     vmem = pl.BlockSpec(memory_space=pltpu.VMEM)
     smem = pl.BlockSpec(memory_space=pltpu.SMEM)
-    exchanges = 2 * ITERS
-    big = pltpu.VMEM((count * 24, LANES), jnp.float32)
-    stress, stored = pl.pallas_call(
-        functools.partial(elastic_kernel, full_x, full_y),
-        out_shape=(
-            jax.ShapeDtypeStruct((6, full_z, cells), jnp.float32),
-            jax.ShapeDtypeStruct((4, full_z, cells), jnp.float32),
-        ),
-        in_specs=[vmem, smem, smem] + [vmem] * 6,
-        out_specs=(vmem, vmem),
+    scratch = lambda *shape: pltpu.VMEM(shape, jnp.float32)
+    buffers = []
+    for _ in range(2 * ITERS):
+        for group in GROUPS:
+            rows = 4 * (group[1] - group[0]) * count
+            buffers += [scratch(rows, LANES), scratch(rows, LANES)]
+            buffers += [pltpu.SemaphoreType.DMA((count,))] * 2
+    x_face = scratch(full_z + full_z * size_y // LANES, LANES)
+    y_face = scratch(full_z, LANES)
+    buffers += [x_face, x_face, y_face, y_face] * 2 + [pltpu.SemaphoreType.DMA((4,))] * 2
+    whole = lambda *lead: jax.ShapeDtypeStruct(lead + (full_z, cells), jnp.float32)
+    result = pl.pallas_call(
+        functools.partial(step_kernel, full_x, full_y),
+        out_shape=(whole(4), whole(), whole(6)),
+        in_specs=[vmem] * 3 + [smem] * 5 + [vmem] * 6,
+        out_specs=(vmem, vmem, vmem),
         scratch_shapes=[
-            pltpu.VMEM((8, full_z, cells), jnp.float32),
-            pltpu.VMEM((6, full_z, cells), jnp.float32),
-            pltpu.VMEM((6, full_z, cells), jnp.float32),
+            scratch(4, full_z, cells),
+            scratch(full_z, cells),
+            scratch(full_z, cells),
+            scratch(4, full_z, cells),
+            scratch(8, full_z, cells),
+            scratch(6, full_z, cells),
+            scratch(6, full_z, cells),
+            scratch(6 * full_x, 2 * full_y),
+            scratch(4, full_x, 2 * full_y),
         ]
-        + [big] * (2 * exchanges)
-        + [pltpu.SemaphoreType.DMA((count,))] * (2 * exchanges),
+        + buffers,
         compiler_params=pltpu.CompilerParams(
             collective_id=0, has_side_effects=True, vmem_limit_bytes=40 * 1024 * 1024
         ),
-    )(spread, lame, eigen, *tables)
-    place = lambda x: x.transpose(0, 2, 1).reshape((-1, size_x, size_y, full_z))
-    return place(stress), place(stored)
+    )(
+        labels.reshape(cells, full_z), seed_noise.reshape(4, cells, full_z),
+        conc.reshape(cells, full_z), curvature, quartic, wells, lame, eigen, *tables
+    )
+    place = lambda x: jnp.swapaxes(x, -1, -2).reshape(x.shape[:-2] + (size_x, size_y, full_z))
+    return tuple(place(x) for x in result)
 
 
 def laplace_padded(padded):
@@ -638,6 +873,13 @@
 
 
 def shards(labels, seed_noise, conc, curvature, quartic, wells, lame, eigen):
+    full_x = labels.shape[0] * lax.axis_size("gx")
+    full_y = labels.shape[1] * lax.axis_size("gy")
+    full_z = labels.shape[2]
+    if kernel_fits(labels.shape):
+        return step_call(
+            labels, seed_noise, conc, curvature, quartic, wells, lame, eigen, full_x, full_y
+        )
     phase = phases_from(labels, seed_noise)
     part, chem = partition(phase, conc, curvature, quartic, wells)
     stacked = jnp.concatenate([phase, chem[None]], axis=0)
@@ -647,34 +889,28 @@
     eigen_field = jnp.einsum("ap,axyz->pxyz", eigen, phase, precision=lax.Precision.HIGHEST)
     lam0 = 0.5 * (jnp.max(lame[0]) + jnp.min(lame[0]))
     mu0 = 0.5 * (jnp.max(lame[1]) + jnp.min(lame[1]))
-    full_x = labels.shape[0] * lax.axis_size("gx")
-    full_y = labels.shape[1] * lax.axis_size("gy")
-    full_z = labels.shape[2]
-    if kernel_fits(labels.shape):
-        stress, stored = elastic_call(phase, lame, eigen, full_x, full_y)
-    else:
-        strain = jnp.zeros((6,) + labels.shape, jnp.float32)
-        step = fluctuation if slots_fit(full_z) else fluctuation_general
-        for _ in range(ITERS):
-            stress = stress_of(strain, eigen_field, lam_field, shear_field)
-            strain = strain - step(stress, full_x, full_y, full_z, lam0, mu0)
+    strain = jnp.zeros((6,) + labels.shape, jnp.float32)
+    step = fluctuation if slots_fit(full_z) else fluctuation_general
+    for _ in range(ITERS):
         stress = stress_of(strain, eigen_field, lam_field, shear_field)
-        elastic = strain - eigen_field
-        trace = elastic[0] + elastic[1] + elastic[2]
-        squares = (
-            elastic[0] ** 2
-            + elastic[1] ** 2
-            + elastic[2] ** 2
-            + 2.0 * (elastic[3] ** 2 + elastic[4] ** 2 + elastic[5] ** 2)
-        )
-        weight = jnp.array([1.0, 1.0, 1.0, 2.0, 2.0, 2.0], jnp.float32)
-        coupling = jnp.einsum(
-            "ap,pxyz->axyz", eigen * weight[None], stress, precision=lax.Precision.HIGHEST
-        )
-        stored = (
-            0.5 * (column(lame[0]) * trace[None] ** 2 + 2.0 * column(lame[1]) * squares[None])
-            - coupling
-        )
+        strain = strain - step(stress, full_x, full_y, full_z, lam0, mu0)
+    stress = stress_of(strain, eigen_field, lam_field, shear_field)
+    elastic = strain - eigen_field
+    trace = elastic[0] + elastic[1] + elastic[2]
+    squares = (
+        elastic[0] ** 2
+        + elastic[1] ** 2
+        + elastic[2] ** 2
+        + 2.0 * (elastic[3] ** 2 + elastic[4] ** 2 + elastic[5] ** 2)
+    )
+    weight = jnp.array([1.0, 1.0, 1.0, 2.0, 2.0, 2.0], jnp.float32)
+    coupling = jnp.einsum(
+        "ap,pxyz->axyz", eigen * weight[None], stress, precision=lax.Precision.HIGHEST
+    )
+    stored = (
+        0.5 * (column(lame[0]) * trace[None] ** 2 + 2.0 * column(lame[1]) * squares[None])
+        - coupling
+    )
     deviate = part - column(wells)
     energy = 0.5 * column(curvature) * deviate**2 + 0.25 * column(quartic) * deviate**4
     chemical = energy - chem[None] * part

time: 89.3 us -> 77.2 us (0.86)
  other arithmetic: 16.4 us -> 0 us
  local copies, waits for them, and re-layouts: 3.96 us -> 11.6 us
  starting transfers between devices: 6.99 us -> 0 us
  Pallas kernels: 57.7 us -> 64.4 us
  waiting for transfers between devices: 3.08 us -> 0 us
    reduce_sum x8 -> x0, other arithmetic: 7.15 us -> none  [the longest x5 5.07 us: partition(): jnp.sum(phase * part, axis=0)]
    unnamed x52 -> x28, local copies, waits for them, and re-layouts: 1.61 us -> 8.74 us
    ppermute x4 -> x0, starting transfers between devices: 6.99 us -> none  [the longest x2 6.99 us: with_halo(): after = lax.ppermute(initial, axis, down)]
    pallas_call x1, Pallas kernels: 57.7 us -> 64.4 us  [step_call(): pl.pallas_call(functools.partial(step_kernel, full_x, full_y), out_shape=...]
    add x7 -> x0, other arithmetic: 3.36 us -> none  [the longest x1 1.75 us: laplace_padded(): total = total + jnp.roll(centre, 1, 3) + jnp.roll(centre, -1, 3)]
    ppermute x4 -> x0, waiting for transfers between devices: 3.08 us -> none  [the longest x2 2.71 us: with_halo(): before = lax.ppermute(last, axis, up)]
    concatenate x3 -> x0, other arithmetic: 2.45 us -> none  [shards(): stacked = jnp.concatenate([phase, chem[None]], axis=0)]
    mul x2 -> x0, other arithmetic: 1.88 us -> none  [the longest x1 1.3 us: shards(): 0.25 * column(quartic) * deviate ** 4]
  transfers between devices with their start and end apart: 4 -> 0, of which waited for: 2 -> 0; matrix products, arithmetic and copies ran while one was open for 6% -> 0% of each run, Pallas kernels for 65% -> 0%
where the time goes in v2:
time: 77.2 us; the launch traced here: 76.7 us
  Pallas kernels  64.4 us (83%)
  local copies, waits for them, and re-layouts  11.6 us (15%)
    pallas_call x1, Pallas kernels, step_call(): pl.pallas_call(functools.partial(step_kernel, full_x, full_y), out_shape=...  64.4 us
    unnamed x28, local copies, waits for them, and re-layouts  8.74 us
    transpose x3, local copies, waits for them, and re-layouts, step_call(): jnp.swapaxes(x, -1, -2).reshape(x.shape[:-2] + (size_x, size_y, full_z))  2.91 us

profile of v2, /device:TPU:0, one launch (start us, length us, event | category | flops | bytes accessed | tf_op | source)
XLA Modules:
  0.0 76.7 jit_solution(925721868374392092)
XLA Ops:
  0.6 0.0 copy-start.12
  0.6 0.0 copy-start.13
  0.7 0.0 copy-start.9
  0.7 0.0 copy-start.10
  0.7 0.0 copy-start.11
  0.7 0.6 copy-done.12
  1.3 0.0 copy-done.13
  1.3 0.0 copy-done.9
  1.3 0.0 copy-done.10
  1.4 0.0 copy-done.11
  1.4 0.0 copy-start
  1.4 1.0 %copy-done = f32[4,8,32,64]{3,2,1,0:T(8,128)S(1)} copy-done((f32[4,8,32,64]{3,2,1,0:T(8,128)S(1)}, f32[4,8,32,64]{3,2,1,0:T(8,128)}, u32[]{:S(2)}) %copy-start) | copy-done | bytes 262168
  2.4 0.0 copy-start.1
  2.4 0.9 %copy-done.1 = bf16[2,256,256]{2,1,0:T(8,128)(2,1)S(1)} copy-done((bf16[2,256,256]{2,1,0:T(8,128)(2,1)S(1)}, bf16[2,256,256]{2,1,0:T(8,128)(2,1)}, u32[]{:S(2)}) %copy-start.1) | copy-done | bytes 262168
  3.4 0.0 copy-start.2
  3.4 0.9 %copy-done.2 = bf16[2,256,256]{2,1,0:T(8,128)(2,1)S(1)} copy-done((bf16[2,256,256]{2,1,0:T(8,128)(2,1)S(1)}, bf16[2,256,256]{2,1,0:T(8,128)(2,1)}, u32[]{:S(2)}) %copy-start.2) | copy-done | bytes 262168
  4.3 0.0 copy-start.3
  4.3 0.9 %copy-done.3 = s32[8,32,64]{2,1,0:T(8,128)S(1)} copy-done((s32[8,32,64]{2,1,0:T(8,128)S(1)}, s32[8,32,64]{2,1,0:T(8,128)}, u32[]{:S(2)}) %copy-start.3) | copy-done | bytes 65560
  5.2 0.0 copy-start.4
  5.2 0.9 %copy-done.4 = f32[8,32,64]{2,1,0:T(8,128)S(1)} copy-done((f32[8,32,64]{2,1,0:T(8,128)S(1)}, f32[8,32,64]{2,1,0:T(8,128)}, u32[]{:S(2)}) %copy-start.4) | copy-done | bytes 65560
  6.1 0.0 copy-start.5
  6.1 0.9 %copy-done.5 = bf16[128,384]{1,0:T(8,128)(2,1)S(1)} copy-done((bf16[128,384]{1,0:T(8,128)(2,1)S(1)}, bf16[128,384]{1,0:T(8,128)(2,1)}, u32[]{:S(2)}) %copy-start.5) | copy-done | bytes 98328
  7.0 0.0 copy-start.6
  7.0 0.9 %copy-done.6 = bf16[128,384]{1,0:T(8,128)(2,1)S(1)} copy-done((bf16[128,384]{1,0:T(8,128)(2,1)S(1)}, bf16[128,384]{1,0:T(8,128)(2,1)}, u32[]{:S(2)}) %copy-start.6) | copy-done | bytes 98328
  7.9 0.0 copy-start.7
  7.9 0.8 copy-done.7
  8.7 0.0 copy-start.8
  8.7 0.8 copy-done.8
  9.4 64.4 %shard_map.157 = (f32[4,64,256]{2,1,0:T(8,128)S(1)}, f32[64,256]{1,0:T(8,128)S(1)}, f32[6,64,256]{2,1,0:T(8,128)S(1)}) custom-call(s32[256,64]{1,0:T(8,128)S(1)} %bitcast.12, f32[4,256,64]{2,1,0:T(8,128)S(1)} %bitcast.9, f32[256,64]{1,0:T(8,128)S(1)} %bitcast.13, f32[4]{0:T(128)S(1)} %copy-done.11, f32[4]{0:T(128)S(1)} %copy-done.12, f32[4]{0:T(128)S(1)} %copy-done.13, ...), custom_call_target="tpu_custom_call" | custom-call | tf_op jit(solution)/shard_map/pallas_call | solution.py:838
  73.8 1.2 %copy.22 = f32[6,256,64]{2,1,0:T(8,128)} copy(f32[6,256,64]{1,2,0:T(8,128)S(1)} %bitcast.10) | data formatting | bytes 786432 | tf_op jit(solution)/shard_map/transpose | solution.py:862
  75.0 1.0 %copy.20 = f32[4,256,64]{2,1,0:T(8,128)} copy(f32[4,256,64]{1,2,0:T(8,128)S(1)} %bitcast.11) | data formatting | bytes 524288 | tf_op jit(solution)/shard_map/transpose | solution.py:862
  76.0 0.8 copy.21
Async XLA Ops:
  0.6 0.7 copy-start.12
  0.6 0.7 copy-start.13
  0.7 0.7 copy-start.9
  0.7 0.7 copy-start.10
  0.7 0.7 copy-start.11
  1.4 1.0 %copy-start = (f32[4,8,32,64]{3,2,1,0:T(8,128)S(1)}, f32[4,8,32,64]{3,2,1,0:T(8,128)}, u32[]{:S(2)}) copy-start(f32[4,8,32,64]{3,2,1,0:T(8,128)} %param.15) | copy-start | bytes 786436
  2.4 0.9 %copy-start.1 = (bf16[2,256,256]{2,1,0:T(8,128)(2,1)S(1)}, bf16[2,256,256]{2,1,0:T(8,128)(2,1)}, u32[]{:S(2)}) copy-start(bf16[2,256,256]{2,1,0:T(8,128)(2,1)} %constant.14.clone.fy_ref) | copy-start | bytes 786436
  3.4 0.9 %copy-start.2 = (bf16[2,256,256]{2,1,0:T(8,128)(2,1)S(1)}, bf16[2,256,256]{2,1,0:T(8,128)(2,1)}, u32[]{:S(2)}) copy-start(bf16[2,256,256]{2,1,0:T(8,128)(2,1)} %constant.15.clone.iy_ref) | copy-start | bytes 786436
  4.3 0.9 %copy-start.3 = (s32[8,32,64]{2,1,0:T(8,128)S(1)}, s32[8,32,64]{2,1,0:T(8,128)}, u32[]{:S(2)}) copy-start(s32[8,32,64]{2,1,0:T(8,128)} %param.14) | copy-start | bytes 196612
  5.2 0.9 %copy-start.4 = (f32[8,32,64]{2,1,0:T(8,128)S(1)}, f32[8,32,64]{2,1,0:T(8,128)}, u32[]{:S(2)}) copy-start(f32[8,32,64]{2,1,0:T(8,128)} %param.16) | copy-start | bytes 196612
  6.1 0.9 %copy-start.5 = (bf16[128,384]{1,0:T(8,128)(2,1)S(1)}, bf16[128,384]{1,0:T(8,128)(2,1)}, u32[]{:S(2)}) copy-start(bf16[128,384]{1,0:T(8,128)(2,1)} %constant.13.clone.fx_ref) | copy-start | bytes 294916
  7.0 0.9 %copy-start.6 = (bf16[128,384]{1,0:T(8,128)(2,1)S(1)}, bf16[128,384]{1,0:T(8,128)(2,1)}, u32[]{:S(2)}) copy-start(bf16[128,384]{1,0:T(8,128)(2,1)} %constant.16.clone.ix_ref) | copy-start | bytes 294916
  7.9 0.8 copy-start.7
  8.7 0.8 copy-start.8

commit v3 on v2

--- a/solution.py
+++ b/solution.py
@@ -338,22 +338,27 @@
     return lax.axis_index("gx") * lax.axis_size("gy") + lax.axis_index("gy")
 
 
-def coordinates(index):
-    count_y = lax.axis_size("gy")
-    return (index // count_y, index % count_y)
+def for_others(action):
+    count_x, count_y = lax.axis_size("gx"), lax.axis_size("gy")
+    i, j = lax.axis_index("gx"), lax.axis_index("gy")
+    turns = [j] + [lax.rem(j + step, count_y) for step in range(1, count_y)]
+    for other in turns[1:]:
+        action(i, other)
+
+    def row(step, carry):
+        far = lax.rem(i + step, count_x)
+        for other in turns:
+            action(far, other)
+        return carry
+
+    lax.fori_loop(1, count_x, row, 0)
 
 
 def greet():
-    count = lax.axis_size("gx") * lax.axis_size("gy")
-    me = position()
     barrier = pltpu.get_barrier_semaphore()
-
-    def hello(step, carry):
-        other = lax.rem(me + step, count)
-        pl.semaphore_signal(barrier, inc=1, device_id=coordinates(other), device_id_type=MESH)
-        return carry
-
-    lax.fori_loop(1, count, hello, 0)
+    for_others(
+        lambda i, j: pl.semaphore_signal(barrier, inc=1, device_id=(i, j), device_id_type=MESH)
+    )
 
 
 def greeted():
@@ -361,47 +366,45 @@
     pl.semaphore_wait(pltpu.get_barrier_semaphore(), count - 1)
 
 
-def exchange_copy(pack, source, target):
+def exchange_start(pack):
     sent, received, send_sem, recv_sem = pack
-    rows = sent.shape[0] // (lax.axis_size("gx") * lax.axis_size("gy"))
+    count_y = lax.axis_size("gy")
+    rows = sent.shape[0] // (lax.axis_size("gx") * count_y)
+    own = pl.ds(pl.multiple_of(position() * rows, 8), rows)
+
+    def send(i, j):
+        pltpu.make_async_remote_copy(
+            src_ref=sent.at[pl.ds(pl.multiple_of((i * count_y + j) * rows, 8), rows)],
+            dst_ref=received.at[own],
+            send_sem=send_sem,
+            recv_sem=recv_sem,
+            device_id=(i, j),
+            device_id_type=MESH,
+        ).start()
+
+    for_others(send)
+    received[own, :] = sent[own, :]
+
+
+def exchange_all(pack):
+    sent, received, send_sem, recv_sem = pack
+    count_x, count_y = lax.axis_size("gx"), lax.axis_size("gy")
+    rows = sent.shape[0] // (count_x * count_y) * (count_x * count_y - 1)
     return pltpu.make_async_remote_copy(
-        src_ref=sent.at[pl.ds(pl.multiple_of(target * rows, 8), rows)],
-        dst_ref=received.at[pl.ds(pl.multiple_of(source * rows, 8), rows)],
-        send_sem=send_sem.at[target],
-        recv_sem=recv_sem.at[source],
-        device_id=coordinates(target),
+        src_ref=sent.at[pl.ds(0, rows)],
+        dst_ref=received.at[pl.ds(0, rows)],
+        send_sem=send_sem,
+        recv_sem=recv_sem,
+        device_id=(lax.rem(lax.axis_index("gx") + 1, count_x), lax.axis_index("gy")),
         device_id_type=MESH,
     )
 
 
-def exchange_start(pack):
-    sent, received = pack[:2]
-    count = lax.axis_size("gx") * lax.axis_size("gy")
-    me = position()
-    rows = sent.shape[0] // count
-
-    def send(step, carry):
-        exchange_copy(pack, me, lax.rem(me + step, count)).start()
-        return carry
-
-    lax.fori_loop(1, count, send, 0)
-    own = pl.ds(pl.multiple_of(me * rows, 8), rows)
-    received[own, :] = sent[own, :]
-
-
 def exchange_wait(pack, arrived):
-    count = lax.axis_size("gx") * lax.axis_size("gy")
-    me = position()
-
-    def wait(step, carry):
-        other = lax.rem(me + step, count)
-        if arrived:
-            exchange_copy(pack, other, other).wait_recv()
-        else:
-            exchange_copy(pack, me, other).wait_send()
-        return carry
-
-    lax.fori_loop(1, count, wait, 0)
+    if arrived:
+        exchange_all(pack).wait_recv()
+    else:
+        exchange_all(pack).wait_send()
 
 
 def swap_blocks(parts):
@@ -669,9 +672,10 @@
 
 
 def step_kernel(
-    full_x, full_y, labels_ref, noise_ref, raw_conc_ref, curve_ref, quart_ref, wells_ref, lame_ref,
-    eigen_ref, mz_ref, fx_ref, fy_ref, iy_ref, ix_ref, wz_ref,
+    full_x, full_y, labels_in, noise_in, raw_conc_in, curve_ref, quart_ref, wells_ref, lame_ref,
+    eigen_ref, mz_in, fx_in, fy_in, iy_in, ix_in, wz_in,
     next_ref, conc_next_ref, stress_ref,
+    labels_ref, noise_ref, raw_conc_ref, mz_ref, fx_ref, fy_ref, iy_ref, ix_ref, wz_ref, load_sem,
     phase_ref, conc_ref, chem_ref, local_ref, field_ref, strain_ref, t_ref, plane_ref, wave_ref,
     *buffers
 ):
@@ -683,7 +687,19 @@
     packs = [packs[n:n + len(GROUPS)] for n in range(0, number, len(GROUPS))]
     halo_sent, halo_got = buffers[4 * number:4 * number + 4], buffers[4 * number + 4:4 * number + 8]
     halo_send, halo_recv = buffers[4 * number + 8:]
+    loads = [
+        pltpu.make_async_copy(source, target, load_sem.at[n])
+        for n, (source, target) in enumerate((
+            (noise_in, noise_ref), (labels_in, labels_ref), (raw_conc_in, raw_conc_ref),
+            (mz_in, mz_ref), (fx_in, fx_ref), (fy_in, fy_ref), (iy_in, iy_ref), (ix_in, ix_ref),
+            (wz_in, wz_ref),
+        ))
+    ]
+    for load in loads:
+        load.start()
     greet()
+    for load in loads[:3]:
+        load.wait()
 
     for h in range(2):
         at = pl.ds(h * LANES, LANES)
@@ -755,6 +771,8 @@
         halo_pack(phase_ref, chem_ref, *halo_sent, width)
         for copy in halo_copies():
             copy.start()
+        for load in loads[4:]:
+            load.wait()
 
     def beside_second():
         for copy in halo_copies():
@@ -771,6 +789,8 @@
     for turn in range(ITERS):
         there, back = packs[2 * turn], packs[2 * turn + 1]
         lax.fori_loop(0, chunks, stresses if turn else fields, 0)
+        if turn == 0:
+            loads[3].wait()
         for pack, group in zip(there, GROUPS):
             halves(mz_ref, t_ref, pack[0], group)
             if turn == 0 and group is GROUPS[0]:
@@ -824,13 +844,14 @@
     tables = [jnp.asarray(t) for t in kernel_tables(size_x, full_x, full_y, full_z)]
     vmem = pl.BlockSpec(memory_space=pltpu.VMEM)
     smem = pl.BlockSpec(memory_space=pltpu.SMEM)
+    hbm = pl.BlockSpec(memory_space=pltpu.HBM)
     scratch = lambda *shape: pltpu.VMEM(shape, jnp.float32)
     buffers = []
     for _ in range(2 * ITERS):
         for group in GROUPS:
             rows = 4 * (group[1] - group[0]) * count
             buffers += [scratch(rows, LANES), scratch(rows, LANES)]
-            buffers += [pltpu.SemaphoreType.DMA((count,))] * 2
+            buffers += [pltpu.SemaphoreType.DMA] * 2
     x_face = scratch(full_z + full_z * size_y // LANES, LANES)
     y_face = scratch(full_z, LANES)
     buffers += [x_face, x_face, y_face, y_face] * 2 + [pltpu.SemaphoreType.DMA((4,))] * 2
@@ -838,9 +859,13 @@
     result = pl.pallas_call(
         functools.partial(step_kernel, full_x, full_y),
         out_shape=(whole(4), whole(), whole(6)),
-        in_specs=[vmem] * 3 + [smem] * 5 + [vmem] * 6,
+        in_specs=[hbm] * 3 + [smem] * 5 + [hbm] * 6,
         out_specs=(vmem, vmem, vmem),
-        scratch_shapes=[
+        scratch_shapes=[pltpu.VMEM((cells, full_z), jnp.int32)]
+        + [scratch(4, cells, full_z), scratch(cells, full_z)]
+        + [pltpu.VMEM(table.shape, table.dtype) for table in tables]
+        + [pltpu.SemaphoreType.DMA((3 + len(tables),))]
+        + [
             scratch(4, full_z, cells),
             scratch(full_z, cells),
             scratch(full_z, cells),
@@ -853,7 +878,7 @@
         ]
         + buffers,
         compiler_params=pltpu.CompilerParams(
-            collective_id=0, has_side_effects=True, vmem_limit_bytes=40 * 1024 * 1024
+            collective_id=0, has_side_effects=True, vmem_limit_bytes=56 * 1024 * 1024
         ),
     )(
         labels.reshape(cells, full_z), seed_noise.reshape(4, cells, full_z),

time: 77.2 us -> 63 us (0.82)
  local copies, waits for them, and re-layouts: 11.6 us -> 3.95 us
  Pallas kernels: 64.4 us -> 58.2 us
    unnamed x28 -> x4, local copies, waits for them, and re-layouts: 8.74 us -> 0.01 us
    pallas_call x1, Pallas kernels: 64.4 us -> 58.2 us  [step_call(): pl.pallas_call(functools.partial(step_kernel, full_x, full_y), out_shape=...]
    transpose x3, local copies, waits for them, and re-layouts: 2.91 us -> 3.94 us  [step_call(): jnp.swapaxes(x, -1, -2).reshape(x.shape[:-2] + (size_x, size_y, full_z))]
where the time goes in v3:
time: 63 us; the launch traced here: 62.8 us
  Pallas kernels  58.2 us (92%)
  local copies, waits for them, and re-layouts  3.95 us (6%)
  between operations  0.65 us (1%)
    pallas_call x1, Pallas kernels, step_call(): pl.pallas_call(functools.partial(step_kernel, full_x, full_y), out_shape=...  58.2 us
    transpose x3, local copies, waits for them, and re-layouts, step_call(): jnp.swapaxes(x, -1, -2).reshape(x.shape[:-2] + (size_x, size_y, full_z))  3.94 us

profile of v3, /device:TPU:0, one launch (start us, length us, event | category | flops | bytes accessed | tf_op | source)
XLA Modules:
  0.0 62.8 jit_solution(16440697907683304972)
XLA Ops:
  0.6 58.2 %shard_map.157 = (f32[4,64,256]{2,1,0:T(8,128)}, f32[64,256]{1,0:T(8,128)}, f32[6,64,256]{2,1,0:T(8,128)}) custom-call(s32[256,64]{1,0:T(8,128)} %bitcast.14, f32[4,256,64]{2,1,0:T(8,128)} %bitcast.11, f32[256,64]{1,0:T(8,128)} %bitcast.15, f32[4]{0:T(128)} %curve_ref.1, f32[4]{0:T(128)} %quart_ref.1, f32[4]{0:T(128)} %wells_ref.1, f32[2,4]{1,0:T(2,128)} %lame_ref.1, ...), custom_call_target="tpu_custom_call" | custom-call | tf_op jit(solution)/shard_map/pallas_call | solution.py:859
  58.8 0.0 copy-start
  58.9 2.2 %copy.22 = f32[6,256,64]{2,1,0:T(8,128)} copy(f32[6,256,64]{1,2,0:T(8,128)} %bitcast.12) | data formatting | bytes 786432 | tf_op jit(solution)/shard_map/transpose | solution.py:887
  61.0 0.0 copy-done
  61.0 0.0 copy-start.1
  61.0 1.0 %copy.20 = f32[4,256,64]{2,1,0:T(8,128)} copy(f32[4,256,64]{1,2,0:T(8,128)S(1)} %bitcast.13) | data formatting | bytes 524288 | tf_op jit(solution)/shard_map/transpose | solution.py:887
  62.0 0.0 copy-done.1
  62.0 0.8 %copy.21 = f32[256,64]{1,0:T(8,128)} copy(f32[256,64]{0,1:T(8,128)S(1)} %bitcast.17) | data formatting | bytes 131072 | tf_op jit(solution)/shard_map/transpose | solution.py:887
Async XLA Ops:
  58.8 2.2 %copy-start = (f32[4,64,256]{2,1,0:T(8,128)S(1)}, f32[4,64,256]{2,1,0:T(8,128)}, u32[]{:S(2)}) copy-start(f32[4,64,256]{2,1,0:T(8,128)} %get-tuple-element.6) | copy-start | bytes 786436
  61.0 1.0 %copy-start.1 = (f32[64,256]{1,0:T(8,128)S(1)}, f32[64,256]{1,0:T(8,128)}, u32[]{:S(2)}) copy-start(f32[64,256]{1,0:T(8,128)} %get-tuple-element.7) | copy-start | bytes 196612

commit v4 on v3

--- a/solution.py
+++ b/solution.py
@@ -422,7 +422,9 @@
     return result
 
 
-GROUPS = ((0, 4), (4, 6))
+GROUPS_THERE = ((0, 4), (4, 6))
+GROUPS_BACK = ((0, 2), (2, 6))
+GROUPS = (GROUPS_THERE, GROUPS_BACK)
 
 
 def halves(z_ref, t_ref, sent, group):
@@ -682,9 +684,9 @@
     full_z = phase_ref.shape[1]
     chunks = full_z // ROWS
     width = full_y // lax.axis_size("gy")
-    number = 2 * ITERS * len(GROUPS)
-    packs = [buffers[4 * n:4 * n + 4] for n in range(number)]
-    packs = [packs[n:n + len(GROUPS)] for n in range(0, number, len(GROUPS))]
+    number = ITERS * (len(GROUPS_THERE) + len(GROUPS_BACK))
+    free = iter([buffers[4 * n:4 * n + 4] for n in range(number)])
+    packs = [[next(free) for _ in GROUPS[t % 2]] for t in range(2 * ITERS)]
     halo_sent, halo_got = buffers[4 * number:4 * number + 4], buffers[4 * number + 4:4 * number + 8]
     halo_send, halo_recv = buffers[4 * number + 8:]
     loads = [
@@ -791,23 +793,23 @@
         lax.fori_loop(0, chunks, stresses if turn else fields, 0)
         if turn == 0:
             loads[3].wait()
-        for pack, group in zip(there, GROUPS):
+        for pack, group in zip(there, GROUPS_THERE):
             halves(mz_ref, t_ref, pack[0], group)
-            if turn == 0 and group is GROUPS[0]:
+            if turn == 0 and group is GROUPS_THERE[0]:
                 greeted()
             exchange_start(pack)
         if turn == 0:
             beside_first()
-        for pack, group in zip(there, GROUPS):
+        for pack, group in zip(there, GROUPS_THERE):
             exchange_wait(pack, True)
             plane_forward(pack[1], plane_ref, fx_ref, fy_ref, group, full_x, full_y)
         plane_green(plane_ref, wave_ref, full_x, full_z)
-        for pack, group in zip(back, GROUPS):
+        for pack, group in zip(back, GROUPS_BACK):
             plane_back(plane_ref, pack[0], iy_ref, ix_ref, group, full_x, full_y)
             exchange_start(pack)
         if turn == 0:
             beside_second()
-        for pack, group in zip(back, GROUPS):
+        for pack, group in zip(back, GROUPS_BACK):
             exchange_wait(pack, True)
             strain_update(pack[1], wz_ref, strain_ref, group)
 
@@ -837,6 +839,42 @@
         copy.wait_send()
 
 
+def place_kernel(next_in, conc_in, stress_in, next_out, conc_out, stress_out, got, made, got_sem, made_sem):
+    sources = [stress_in.at[p] for p in range(6)] + [next_in.at[a] for a in range(4)] + [conc_in]
+    targets = [stress_out.at[p] for p in range(6)] + [next_out.at[a] for a in range(4)] + [conc_out]
+    number = len(sources)
+    loads = [pltpu.make_async_copy(sources[n], got.at[n], got_sem.at[n]) for n in range(number)]
+    stores = [pltpu.make_async_copy(made.at[n], targets[n], made_sem.at[n]) for n in range(number)]
+    for load in loads:
+        load.start()
+    for n in range(number):
+        loads[n].wait()
+        for h in range(got.shape[2] // LANES):
+            made[n, half(h), :] = got[n, :, half(h)].T
+        stores[n].start()
+    for store in stores:
+        store.wait()
+
+
+def place_call(phase_next, conc_next, stress):
+    full_z, cells = conc_next.shape
+    hbm = pl.BlockSpec(memory_space=pl.ANY)
+    turned_shape = lambda *lead: jax.ShapeDtypeStruct(lead + (cells, full_z), jnp.float32)
+    return pl.pallas_call(
+        place_kernel,
+        out_shape=(turned_shape(4), turned_shape(), turned_shape(6)),
+        in_specs=[hbm] * 3,
+        out_specs=(hbm,) * 3,
+        scratch_shapes=[
+            pltpu.VMEM((11, full_z, cells), jnp.float32),
+            pltpu.VMEM((11, cells, full_z), jnp.float32),
+            pltpu.SemaphoreType.DMA((11,)),
+            pltpu.SemaphoreType.DMA((11,)),
+        ],
+        compiler_params=pltpu.CompilerParams(vmem_limit_bytes=56 * 1024 * 1024),
+    )(phase_next, conc_next, stress)
+
+
 def step_call(labels, seed_noise, conc, curvature, quartic, wells, lame, eigen, full_x, full_y):
     size_x, size_y, full_z = labels.shape
     cells = size_x * size_y
@@ -847,8 +885,8 @@
     hbm = pl.BlockSpec(memory_space=pltpu.HBM)
     scratch = lambda *shape: pltpu.VMEM(shape, jnp.float32)
     buffers = []
-    for _ in range(2 * ITERS):
-        for group in GROUPS:
+    for t in range(2 * ITERS):
+        for group in GROUPS[t % 2]:
             rows = 4 * (group[1] - group[0]) * count
             buffers += [scratch(rows, LANES), scratch(rows, LANES)]
             buffers += [pltpu.SemaphoreType.DMA] * 2
@@ -884,8 +922,9 @@
         labels.reshape(cells, full_z), seed_noise.reshape(4, cells, full_z),
         conc.reshape(cells, full_z), curvature, quartic, wells, lame, eigen, *tables
     )
-    place = lambda x: jnp.swapaxes(x, -1, -2).reshape(x.shape[:-2] + (size_x, size_y, full_z))
-    return tuple(place(x) for x in result)
+    phase_next, conc_next, stress = place_call(*result)
+    shape = (size_x, size_y, full_z)
+    return phase_next.reshape((4,) + shape), conc_next.reshape(shape), stress.reshape((6,) + shape)
 
 
 def laplace_padded(padded):

time: 63 us -> 61.2 us (0.971)
  local copies, waits for them, and re-layouts: 3.95 us -> 0 us
  Pallas kernels: 58.2 us -> 60.3 us
    transpose x3 -> x0, local copies, waits for them, and re-layouts: 3.94 us -> none  [step_call(): jnp.swapaxes(x, -1, -2).reshape(x.shape[:-2] + (size_x, size_y, full_z))]
    pallas_call x0 -> x1, Pallas kernels: none -> 2.81 us  [place_call(): pl.pallas_call(place_kernel, out_shape=(turned_shape(4), turned_shape(),...]
    pallas_call x1, Pallas kernels: 58.2 us -> 57.5 us  [step_call(): pl.pallas_call(functools.partial(step_kernel, full_x, full_y), out_shape=...]
where the time goes in v4:
time: 61.2 us; the launch traced here: 60.9 us
  Pallas kernels  60.3 us (99%)
  between operations  0.64 us (1%)
    pallas_call x1, Pallas kernels, step_call(): pl.pallas_call(functools.partial(step_kernel, full_x, full_y), out_shape=...  57.5 us
    pallas_call x1, Pallas kernels, place_call(): pl.pallas_call(place_kernel, out_shape=(turned_shape(4), turned_shape(),...  2.81 us

profile of v4, /device:TPU:0, one launch (start us, length us, event | category | flops | bytes accessed | tf_op | source)
XLA Modules:
  0.0 60.9 jit_solution(3501900956643193012)
XLA Ops:
  0.6 57.5 %shard_map.157 = (f32[4,64,256]{2,1,0:T(8,128)}, f32[64,256]{1,0:T(8,128)}, f32[6,64,256]{2,1,0:T(8,128)}) custom-call(s32[256,64]{1,0:T(8,128)} %bitcast.7, f32[4,256,64]{2,1,0:T(8,128)} %bitcast.6, f32[256,64]{1,0:T(8,128)} %bitcast.8, f32[4]{0:T(128)} %curve_ref.1, f32[4]{0:T(128)} %quart_ref.1, f32[4]{0:T(128)} %wells_ref.1, f32[2,4]{1,0:T(2,128)} %lame_ref.1, ...), custom_call_target="tpu_custom_call" | custom-call | tf_op jit(solution)/shard_map/pallas_call | solution.py:897
  58.1 2.8 %shard_map.158 = (f32[4,256,64]{2,1,0:T(8,128)}, f32[256,64]{1,0:T(8,128)}, f32[6,256,64]{2,1,0:T(8,128)}) custom-call(f32[4,64,256]{2,1,0:T(8,128)} %get-tuple-element.9.next_in, f32[64,256]{1,0:T(8,128)} %get-tuple-element.10.conc_in, f32[6,64,256]{2,1,0:T(8,128)} %get-tuple-element.11.stress_in), custom_call_target="tpu_custom_call" | custom-call | tf_op jit(solution)/shard_map/pallas_call | solution.py:863

commit v5 on v4

--- a/solution.py
+++ b/solution.py
@@ -422,9 +422,9 @@
     return result
 
 
-GROUPS_THERE = ((0, 4), (4, 6))
-GROUPS_BACK = ((0, 2), (2, 6))
-GROUPS = (GROUPS_THERE, GROUPS_BACK)
+MAIN = (0, 4)
+PAIR = (4, 6)
+GROUPS = (MAIN, PAIR)
 
 
 def halves(z_ref, t_ref, sent, group):
@@ -684,9 +684,9 @@
     full_z = phase_ref.shape[1]
     chunks = full_z // ROWS
     width = full_y // lax.axis_size("gy")
-    number = ITERS * (len(GROUPS_THERE) + len(GROUPS_BACK))
+    number = 2 * ITERS * len(GROUPS)
     free = iter([buffers[4 * n:4 * n + 4] for n in range(number)])
-    packs = [[next(free) for _ in GROUPS[t % 2]] for t in range(2 * ITERS)]
+    packs = [{group: next(free) for group in GROUPS} for t in range(2 * ITERS)]
     halo_sent, halo_got = buffers[4 * number:4 * number + 4], buffers[4 * number + 4:4 * number + 8]
     halo_send, halo_recv = buffers[4 * number + 8:]
     loads = [
@@ -700,24 +700,26 @@
     for load in loads:
         load.start()
     greet()
-    for load in loads[:3]:
+    for load in loads[:2]:
         load.wait()
 
     for h in range(2):
         at = pl.ds(h * LANES, LANES)
         label = labels_ref[at, :]
         raw = [noise_ref[a, at, :] + jnp.where(label == a, 2.0, 0.0) for a in range(4)]
-        total = raw[0] + raw[1] + raw[2] + raw[3]
         for a in range(4):
-            phase_ref[a, :, half(h)] = (raw[a] / total).T
-        conc_ref[:, half(h)] = raw_conc_ref[at, :].T
+            phase_ref[a, :, half(h)] = raw[a].T
 
     def rows_at(step):
         return pl.ds(pl.multiple_of(step * ROWS, ROWS), ROWS)
 
     def fields(step, carry):
         at = rows_at(step)
-        phase = [phase_ref[a, at, :] for a in range(4)]
+        raw = [phase_ref[a, at, :] for a in range(4)]
+        share = 1.0 / (raw[0] + raw[1] + raw[2] + raw[3])
+        phase = [value * share for value in raw]
+        for a in range(4):
+            phase_ref[a, at, :] = phase[a]
         for which in range(2):
             field_ref[which, at, :] = sum(phase[a] * lame_ref[which, a] for a in range(4))
         for p in range(6):
@@ -728,11 +730,20 @@
             t_ref[p, at, :] = stress[p]
         return carry
 
-    def stresses(step, carry):
+    def main_stresses(step, carry):
         at = rows_at(step)
-        _, _, stress = elastic_chunk(at, strain_ref, field_ref)
-        for p in range(6):
-            t_ref[p, at, :] = stress[p]
+        elastic = [strain_ref[p, at, :] - field_ref[2 + p, at, :] for p in range(4)]
+        spread = field_ref[0, at, :] * (elastic[0] + elastic[1] + elastic[2])
+        shear2 = 2.0 * field_ref[1, at, :]
+        for p in range(4):
+            t_ref[p, at, :] = shear2 * elastic[p] + spread if p < 3 else shear2 * elastic[p]
+        return carry
+
+    def pair_stresses(step, carry):
+        at = rows_at(step)
+        shear2 = 2.0 * field_ref[1, at, :]
+        for p in range(*PAIR):
+            t_ref[p, at, :] = shear2 * (strain_ref[p, at, :] - field_ref[2 + p, at, :])
         return carry
 
     def newton(step, carry):
@@ -767,16 +778,22 @@
         ]
 
     def beside_first():
+        loads[2].wait()
+        for h in range(2):
+            conc_ref[:, half(h)] = raw_conc_ref[pl.ds(h * LANES, LANES), :].T
         for w, value in enumerate(wave_parts(lame_ref, full_x, full_y, full_z)[:4]):
             wave_ref[w] = value
-        lax.fori_loop(0, chunks, newton, 0)
+        lax.fori_loop(0, chunks // 2, newton, 0)
+        for load in loads[4:]:
+            load.wait()
+
+    def beside_second():
+        lax.fori_loop(chunks // 2, chunks, newton, 0)
         halo_pack(phase_ref, chem_ref, *halo_sent, width)
         for copy in halo_copies():
             copy.start()
-        for load in loads[4:]:
-            load.wait()
-
-    def beside_second():
+
+    def beside_third():
         for copy in halo_copies():
             copy.wait_recv()
         for f in range(5):
@@ -788,30 +805,42 @@
                 else:
                     conc_next_ref[:, half(h)] = conc_ref[:, half(h)] + step_conc * spread[h]
 
+    def send_there(turn, group):
+        pack = packs[2 * turn][group]
+        halves(mz_ref, t_ref, pack[0], group)
+        if turn == 0 and group is MAIN:
+            greeted()
+        exchange_start(pack)
+
+    lax.fori_loop(0, chunks, fields, 0)
+    loads[3].wait()
+    send_there(0, MAIN)
+    send_there(0, PAIR)
     for turn in range(ITERS):
         there, back = packs[2 * turn], packs[2 * turn + 1]
-        lax.fori_loop(0, chunks, stresses if turn else fields, 0)
-        if turn == 0:
-            loads[3].wait()
-        for pack, group in zip(there, GROUPS_THERE):
-            halves(mz_ref, t_ref, pack[0], group)
-            if turn == 0 and group is GROUPS_THERE[0]:
-                greeted()
-            exchange_start(pack)
         if turn == 0:
             beside_first()
-        for pack, group in zip(there, GROUPS_THERE):
-            exchange_wait(pack, True)
-            plane_forward(pack[1], plane_ref, fx_ref, fy_ref, group, full_x, full_y)
+        elif turn == 1:
+            beside_third()
+        for group in (PAIR, MAIN) if turn else (MAIN, PAIR):
+            exchange_wait(there[group], True)
+            plane_forward(there[group][1], plane_ref, fx_ref, fy_ref, group, full_x, full_y)
         plane_green(plane_ref, wave_ref, full_x, full_z)
-        for pack, group in zip(back, GROUPS_BACK):
-            plane_back(plane_ref, pack[0], iy_ref, ix_ref, group, full_x, full_y)
-            exchange_start(pack)
+        for group in (PAIR, MAIN):
+            plane_back(plane_ref, back[group][0], iy_ref, ix_ref, group, full_x, full_y)
+            exchange_start(back[group])
         if turn == 0:
             beside_second()
-        for pack, group in zip(back, GROUPS_BACK):
-            exchange_wait(pack, True)
-            strain_update(pack[1], wz_ref, strain_ref, group)
+        exchange_wait(back[PAIR], True)
+        strain_update(back[PAIR][1], wz_ref, strain_ref, PAIR)
+        if turn + 1 < ITERS:
+            lax.fori_loop(0, chunks, pair_stresses, 0)
+            send_there(turn + 1, PAIR)
+        exchange_wait(back[MAIN], True)
+        strain_update(back[MAIN][1], wz_ref, strain_ref, MAIN)
+        if turn + 1 < ITERS:
+            lax.fori_loop(0, chunks, main_stresses, 0)
+            send_there(turn + 1, MAIN)
 
     def finish(step, carry):
         at = rows_at(step)
@@ -833,7 +862,7 @@
 
     lax.fori_loop(0, chunks, finish, 0)
     for group_packs in packs:
-        for pack in group_packs:
+        for pack in group_packs.values():
             exchange_wait(pack, False)
     for copy in halo_copies():
         copy.wait_send()
@@ -886,7 +915,7 @@
     scratch = lambda *shape: pltpu.VMEM(shape, jnp.float32)
     buffers = []
     for t in range(2 * ITERS):
-        for group in GROUPS[t % 2]:
+        for group in GROUPS:
             rows = 4 * (group[1] - group[0]) * count
             buffers += [scratch(rows, LANES), scratch(rows, LANES)]
             buffers += [pltpu.SemaphoreType.DMA] * 2

time: 61.2 us -> 59.6 us (0.974)
  Pallas kernels: 60.3 us -> 58.8 us
    pallas_call x1, Pallas kernels: 57.5 us -> 56 us  [step_call(): pl.pallas_call(functools.partial(step_kernel, full_x, full_y), out_shape=...]
where the time goes in v5:
time: 59.6 us; the launch traced here: 59.4 us
  Pallas kernels  58.8 us (99%)
  between operations  0.64 us (1%)
    pallas_call x1, Pallas kernels, step_call(): pl.pallas_call(functools.partial(step_kernel, full_x, full_y), out_shape=...  56 us
    pallas_call x1, Pallas kernels, place_call(): pl.pallas_call(place_kernel, out_shape=(turned_shape(4), turned_shape(),...  2.81 us

profile of v5, /device:TPU:0, one launch (start us, length us, event | category | flops | bytes accessed | tf_op | source)
XLA Modules:
  0.0 59.4 jit_solution(8162902014916186146)
XLA Ops:
  0.6 56.0 %shard_map.157 = (f32[4,64,256]{2,1,0:T(8,128)}, f32[64,256]{1,0:T(8,128)}, f32[6,64,256]{2,1,0:T(8,128)}) custom-call(s32[256,64]{1,0:T(8,128)} %bitcast.7, f32[4,256,64]{2,1,0:T(8,128)} %bitcast.6, f32[256,64]{1,0:T(8,128)} %bitcast.8, f32[4]{0:T(128)} %curve_ref.1, f32[4]{0:T(128)} %quart_ref.1, f32[4]{0:T(128)} %wells_ref.1, f32[2,4]{1,0:T(2,128)} %lame_ref.1, ...), custom_call_target="tpu_custom_call" | custom-call | tf_op jit(solution)/shard_map/pallas_call | solution.py:926
  56.6 2.8 %shard_map.158 = (f32[4,256,64]{2,1,0:T(8,128)}, f32[256,64]{1,0:T(8,128)}, f32[6,256,64]{2,1,0:T(8,128)}) custom-call(f32[4,64,256]{2,1,0:T(8,128)} %get-tuple-element.9.next_in, f32[64,256]{1,0:T(8,128)} %get-tuple-element.10.conc_in, f32[6,64,256]{2,1,0:T(8,128)} %get-tuple-element.11.stress_in), custom_call_target="tpu_custom_call" | custom-call | tf_op jit(solution)/shard_map/pallas_call | solution.py:892
